TPU v7x, 128 devices: a whole 4x4x4 slice. The times are simulated.
128 devices in a mesh: row: 8 (over y_lo, z), col: 16 (over x, y_hi, core).
Axes of the slice: x: 4, y: 4 (y_hi: 2, y_lo: 2; y = y_hi * 2 + y_lo), z: 4, core: 2. Of those that a mesh axis runs over, the one named last changes fastest.
Arguments:
- inputs: bfloat16 [12288, 8192], P('row', 'col'), may hold values from -6 to 6
- cotangent: bfloat16 [12288, 8192], P('row', 'col'), may hold values from -6 to 6
- conv_out: bfloat16 [12288, 8192], P('row', 'col'), may hold values from -6 to 6
- pre_act: bfloat16 [12288, 2048], P('row', 'col'), may hold values from -6 to 6
- weight_in: bfloat16 [8192, 2048], P('col', 'row'), may hold values from -0.0625 to 0.0625
- weight_out: bfloat16 [2048, 8192], P('row', 'col'), may hold values from -0.125 to 0.125
- scale_mid: float32 [2048], P('col'), may hold values from 0.3 to 3
- scale_wide: float32 [8192], P('col'), may hold values from 0.3 to 3
- keep_mid: int32 [2048], P('col'), may hold values 0 or 1
- keep_wide: int32 [8192], P('col'), may hold values 0 or 1
Outputs:
- grad_x: bfloat16 [12288, 8192], P('row', 'col')
- grad_win: float32 [8192, 2048], P('col', 'row')
- grad_wout: float32 [2048, 8192], P('row', 'col')
- grad_smid: float32 [2048], P('col')
- grad_swide: float32 [8192], P('col')
All inputs are finite; a program needn't handle non-finite values. No bound on the sum of `keep_mid` or of `keep_wide` on one device may be relied on, other than what follows from the above.
Results may differ from a plain program's by a relative error of at most 0.03.
Values may be sent and summed in bfloat16 or wider, within the bound.
No kernel may reach another device: no remote copies, remote signals or barrier semaphores. Data moves between devices by JAX's collectives and lax.ppermute only.
A program may use at most 128 MiB of HBM per device.

v0:
```python
import math

import jax
import jax.numpy as jnp
from jax import lax
from jax.sharding import PartitionSpec as P


def local(
    inputs,
    cotangent,
    conv_out,
    pre_act,
    weight_in,
    weight_out,
    scale_mid,
    scale_wide,
    keep_mid,
    keep_wide,
):
    row_count = inputs.shape[0]
    scaling = 1.0 / math.sqrt(row_count * lax.axis_size("row"))
    wide_gain = scale_wide * keep_wide.astype(jnp.float32)
    cot_float = cotangent.astype(jnp.float32)
    grad_conv = (cot_float * wide_gain).astype(jnp.bfloat16)
    wide_part = jnp.sum(cot_float * conv_out.astype(jnp.float32), axis=0)
    out_panels = lax.all_gather(weight_out, "row", axis=0, tiled=True)
    grad_hid = (
        lax.psum_scatter(
            lax.dot_general(
                out_panels, grad_conv, (((1,), (1,)), ((), ())), preferred_element_type=jnp.float32
            ).astype(jnp.bfloat16),
            "col",
            scatter_dimension=0,
            tiled=True,
        )
        .astype(jnp.float32)
        .T
    )
    mid_gain = scale_mid * keep_mid.astype(jnp.float32)
    pre_float = pre_act.astype(jnp.float32)
    alive_mask = (pre_act > 0) & (keep_mid > 0)[None, :]
    grad_pre = jnp.where(alive_mask, grad_hid, 0.0)
    mid_part = jnp.sum(grad_pre * pre_float, axis=0)
    hidden = jnp.maximum(pre_float * mid_gain, 0.0).astype(jnp.bfloat16)
    grad_act = (grad_pre * mid_gain).astype(jnp.bfloat16)
    hidden_full, act_grad_full = (
        lax.all_gather(hidden, "col", axis=1, tiled=True),
        lax.all_gather(grad_act, "col", axis=1, tiled=True),
    )
    mid_sum, wide_sum = lax.psum((mid_part, wide_part), "row")
    grad_smid = keep_mid.astype(jnp.float32) * scaling * mid_sum
    grad_swide = keep_wide.astype(jnp.float32) * scaling * wide_sum
    panel = hidden_full
    grad_wout = (
        lax.psum_scatter(
            lax.dot_general(
                panel, grad_conv, (((0,), (0,)), ((), ())), preferred_element_type=jnp.float32
            ).astype(jnp.bfloat16),
            "row",
            scatter_dimension=0,
            tiled=True,
        ).astype(jnp.float32)
        * scaling
    )
    product = lax.dot_general(
        act_grad_full,
        lax.all_gather(weight_in, "row", axis=1, tiled=True),
        (((1,), (1,)), ((), ())),
        preferred_element_type=jnp.float32,
    )
    grad_x = (cot_float + product).astype(jnp.bfloat16)
    panel = act_grad_full
    grad_win = (
        lax.psum_scatter(
            lax.dot_general(
                panel, inputs, (((0,), (0,)), ((), ())), preferred_element_type=jnp.float32
            ).astype(jnp.bfloat16),
            "row",
            scatter_dimension=0,
            tiled=True,
        ).astype(jnp.float32)
        * scaling
    ).T
    return (grad_x, grad_win, grad_wout, grad_smid, grad_swide)


def solution(mesh):
    return jax.shard_map(
        local,
        mesh=mesh,
        in_specs=(
            P("row", "col"),
            P("row", "col"),
            P("row", "col"),
            P("row", "col"),
            P("col", "row"),
            P("row", "col"),
            P("col"),
            P("col"),
            P("col"),
            P("col"),
        ),
        out_specs=(P("row", "col"), P("col", "row"), P("row", "col"), P("col"), P("col")),
        check_vma=False,
    )
```

profile of v0, /device:TPU:0, one launch (start us, length us, event | category | flops | bytes accessed | tf_op | source)
XLA Modules:
  0.0 445.7 jit_solution(5175392563864142702)
XLA Ops:
  7.2 0.7 all-gather.5.cloned.1.call-update
  7.9 0.0 reduce-scatter.10.cloned.1.call-start
  8.0 0.7 convert_multiply_fusion.5
  8.7 45.4 %all-gather.5.cloned.1.call-done = bf16[2048,512]{1,0:T(8,128)(2,1)} async-done(((bf16[256,512]{1,0:T(8,128)(2,1)}), bf16[2048,512]{1,0:T(8,128)(2,1)}) %all-gather.5.cloned.1.call-update) | async-done | bytes 2097168 | tf_op jit(solution)/shard_map/all_gather | solution.py:27
  54.1 8.2 %fusion = bf16[2048,1536]{0,1:T(8,128)(2,1)} fusion(bf16[2048,512]{1,0:T(8,128)(2,1)} %all-gather.5.cloned.1.call-done, bf16[1536,512]{1,0:T(8,128)(2,1)} %param.11, f32[512]{0:T(512)S(1)} %convert_multiply_fusion.5), kind=kOutput, calls=%fused_computation.1 | convolution fusion | flops 3226730496 | bytes 9963520 | tf_op jit(solution)/shard_map/dot_general | solution.py:30
  62.3 8.6 %copy.17 = bf16[2048,1536]{1,0:T(8,128)(2,1)} copy(bf16[2048,1536]{0,1:T(8,128)(2,1)} %fusion) | data formatting | bytes 12582912
  70.9 0.0 all-gather.7.cloned.1.call-start
  71.0 0.6 copy-done.6
  71.6 88.1 %reduce-scatter.10.cloned.1.call-done = bf16[128,1536]{1,0:T(8,128)(2,1)} async-done(((bf16[2048,1536]{1,0:T(8,128)(2,1)}), bf16[128,1536]{1,0:T(8,128)(2,1)}) %reduce-scatter.10.cloned.1.call-update) | async-done | bytes 393232
  159.6 1.2 copy.18
  160.9 1.2 fusion.8
  162.1 0.0 all-gather.11.cloned.1.call-start
  162.2 0.5 all-gather.11.cloned.1.call-update
  162.7 0.5 all-gather.9.cloned.1.call-update
  163.3 0.0 reduce-scatter.6.cloned.1.call-start
  163.3 67.4 %all-gather.7.cloned.1.call-done = bf16[1536,2048]{1,0:T(8,128)(2,1)} async-done(((bf16[1536,128]{1,0:T(8,128)(2,1)}), bf16[1536,2048]{1,0:T(8,128)(2,1)}) %all-gather.7.cloned.1.call-update) | async-done | bytes 6291472 | tf_op jit(solution)/shard_map/all_gather | solution.py:49
  230.7 7.7 %convolution_convert_fusion.2 = bf16[2048,512]{1,0:T(8,128)(2,1)} fusion(bf16[1536,2048]{1,0:T(8,128)(2,1)} %all-gather.7.cloned.1.call-done, bf16[1536,512]{1,0:T(8,128)(2,1)S(1)} %copy-done), kind=kOutput, calls=%fused_computation.9 | convolution fusion | flops 3222274048 | bytes 9961472 | tf_op jit(solution)/shard_map/dot_general | solution.py:76
  238.4 0.0 reduce-scatter.8.cloned.1.call-start
  238.4 63.0 %all-gather.11.cloned.1.call-done = bf16[1536,2048]{1,0:T(8,128)(2,1)} async-done(((bf16[1536,128]{1,0:T(8,128)(2,1)}), bf16[1536,2048]{1,0:T(8,128)(2,1)}) %all-gather.11.cloned.1.call-update) | async-done | bytes 6291472 | tf_op jit(solution)/shard_map/all_gather | solution.py:48
  301.4 7.6 %convolution_convert_fusion.1 = bf16[2048,512]{1,0:T(8,128)(2,1)} fusion(bf16[1536,2048]{1,0:T(8,128)(2,1)} %all-gather.11.cloned.1.call-done, bf16[1536,512]{1,0:T(8,128)(2,1)S(1)} %copy-done.2, f32[512]{0:T(512)S(1)} %convert_multiply_fusion.5), kind=kOutput, calls=%fused_computation.8 | convolution fusion | flops 3224633344 | bytes 9963520 | tf_op jit(solution)/shard_map/dot_general | solution.py:57
  309.1 1.4 copy-done.1
  310.5 1.9 fusion.2
  312.4 19.1 %all-reduce = (f32[128]{0:T(128)S(1)}, f32[512]{0:T(512)S(1)}) all-reduce(f32[128]{0:T(128)S(1)} %get-tuple-element.17, f32[512]{0:T(512)S(1)} %fusion.2), channel_id=1, replica_groups=mesh['row'=8,'col'=16] {'row'}, use_global_device_ids=true, to_apply=%region_4.5 | all-reduce | flops 640 | bytes 5120 | tf_op jit(solution)/shard_map/psum | solution.py:51
  331.5 0.5 multiply_multiply_fusion.1
  332.0 0.6 multiply_multiply_fusion
  332.6 14.4 %all-gather.9.cloned.1.call-done = bf16[512,2048]{1,0:T(8,128)(2,1)} async-done(((bf16[512,256]{1,0:T(8,128)(2,1)}), bf16[512,2048]{1,0:T(8,128)(2,1)}) %all-gather.9.cloned.1.call-update) | async-done | bytes 2097168 | tf_op jit(solution)/shard_map/all_gather | solution.py:68
  347.0 8.4 %fusion.3 = bf16[1536,512]{1,0:T(8,128)(2,1)} fusion(bf16[1536,2048]{1,0:T(8,128)(2,1)} %all-gather.7.cloned.1.call-done, bf16[512,2048]{1,0:T(8,128)(2,1)} %all-gather.9.cloned.1.call-done, bf16[1536,512]{1,0:T(8,128)(2,1)} %param.11), kind=kOutput, calls=%fused_computation.7 | convolution fusion | flops 3223584768 | bytes 11534336 | tf_op jit(solution)/shard_map/dot_general | solution.py:66
  355.4 37.7 %reduce-scatter.6.cloned.1.call-done = bf16[256,512]{1,0:T(8,128)(2,1)} async-done(((bf16[2048,512]{1,0:T(8,128)(2,1)}), bf16[256,512]{1,0:T(8,128)(2,1)}) %reduce-scatter.6.cloned.1.call-update) | async-done | bytes 262160 | tf_op jit(solution)/shard_map/reduce_scatter | solution.py:75
  393.2 1.0 multiply_bitcast_fusion
  394.2 1.0 copy.16
  395.2 41.9 %reduce-scatter.8.cloned.1.call-done = bf16[256,512]{1,0:T(8,128)(2,1)} async-done(((bf16[2048,512]{1,0:T(8,128)(2,1)}), bf16[256,512]{1,0:T(8,128)(2,1)}) %reduce-scatter.8.cloned.1.call-update) | async-done | bytes 262160 | tf_op jit(solution)/shard_map/reduce_scatter | solution.py:56
  437.0 1.8 convert_multiply_fusion.4
  (20 shorter events, 0.2 us)
Async XLA Ops:
  7.2 223.5 %copy-start = (bf16[1536,512]{1,0:T(8,128)(2,1)S(1)}, bf16[1536,512]{1,0:T(8,128)(2,1)}, u32[]{:S(2)}) copy-start(bf16[1536,512]{1,0:T(8,128)(2,1)} %param.10) | copy-start | bytes 4718596
  7.2 46.9 %all-gather.5.cloned.1.call-start = ((), (), s32[]{:S(2)}) async-start(), calls=%async_computation.3 | async-start | bytes 2359296 | tf_op jit(solution)/shard_map/all_gather | solution.py:27
  7.9 151.7 %reduce-scatter.10.cloned.1.call-start = ((), (), s32[]{:S(2)}) async-start(), calls=%async_computation.9 | async-start | bytes 6684672
  70.9 0.7 copy-start.6
  70.9 0.7 copy-start.5
  70.9 90.0 %copy-start.3 = (bf16[1536,128]{1,0:T(8,128)(2,1)S(1)}, bf16[1536,128]{1,0:T(8,128)(2,1)}, u32[]{:S(2)}) copy-start(bf16[1536,128]{1,0:T(8,128)(2,1)} %param.13) | copy-start | bytes 1179652
  70.9 159.8 %all-gather.7.cloned.1.call-start = ((), (), s32[]{:S(2)}) async-start(), calls=%async_computation.4 | async-start | bytes 6684672 | tf_op jit(solution)/shard_map/all_gather | solution.py:49
  162.1 139.3 %all-gather.11.cloned.1.call-start = ((), (), s32[]{:S(2)}) async-start(), calls=%async_computation.7 | async-start | bytes 6684672 | tf_op jit(solution)/shard_map/all_gather | solution.py:48
  162.7 184.3 %all-gather.9.cloned.1.call-start = ((), (), s32[]{:S(2)}) async-start(), calls=%async_computation.5 | async-start | bytes 2359296 | tf_op jit(solution)/shard_map/all_gather | solution.py:68
  163.3 229.9 %reduce-scatter.6.cloned.1.call-start = ((), (), s32[]{:S(2)}) async-start(), calls=%async_computation.6 | async-start | bytes 2359296 | tf_op jit(solution)/shard_map/reduce_scatter | solution.py:75
  238.4 63.0 %copy-start.2 = (bf16[1536,512]{1,0:T(8,128)(2,1)S(1)}, bf16[1536,512]{1,0:T(8,128)(2,1)}, u32[]{:S(2)}) copy-start(bf16[1536,512]{1,0:T(8,128)(2,1)} %param.11) | copy-start | bytes 4718596
  238.4 198.6 %reduce-scatter.8.cloned.1.call-start = ((), (), s32[]{:S(2)}) async-start(), calls=%async_computation.8 | async-start | bytes 2359296 | tf_op jit(solution)/shard_map/reduce_scatter | solution.py:56
  309.1 1.4 copy-start.1
  310.5 21.5 %copy-start.4 = (s32[512]{0:T(512)S(1)}, s32[512]{0:T(512)}, u32[]{:S(2)}) copy-start(s32[512]{0:T(512)} %param.19) | copy-start | bytes 6148
Sparse Core Ops, SparseCore 0:
  9.7 44.3 all-gather.4
  71.0 88.5 reduce-scatter.9
  162.5 68.1 all-gather.6
  233.4 67.9 all-gather.10
  302.8 44.1 all-gather.8
  349.2 43.8 reduce-scatter.5
  395.6 41.4 reduce-scatter.7
where the time goes:
time: 446 us
  waiting for transfers between devices  360 us (81%)
  matrix products  31.9 us (7%)
  blocking collectives  19.1 us (4%)
  between operations  14.2 us (3%)
  local copies, waits for them, and re-layouts  12.9 us (3%)
  other arithmetic  7.77 us (2%)
    unnamed x8, waiting for transfers between devices  89.9 us
    all_gather x1, waiting for transfers between devices, local(): lax.all_gather(grad_act, 'col', axis=1, tiled=True)  67.4 us
    all_gather x1, waiting for transfers between devices, local(): lax.all_gather(hidden, 'col', axis=1, tiled=True)  63 us
    all_gather x1, waiting for transfers between devices, local(): out_panels = lax.all_gather(weight_out, 'row', axis=0, tiled=True)  45.4 us
    reduce_scatter x1, waiting for transfers between devices, local(): lax.psum_scatter(lax.dot_general(panel, grad_conv, (((0,), (0,)), ((), ()...  41.9 us
    reduce_scatter x1, waiting for transfers between devices, local(): lax.psum_scatter(lax.dot_general(panel, inputs, (((0,), (0,)), ((), ())),...  37.7 us
    psum x1, blocking collectives, local(): mid_sum, wide_sum = lax.psum((mid_part, wide_part), 'row')  19.1 us
    all_gather x1, waiting for transfers between devices, local(): lax.all_gather(weight_in, 'row', axis=1, tiled=True)  14.4 us
  transfers between devices with their start and end apart: 7, of which 7 were waited for; matrix products, arithmetic and copies ran while one was open for 7% of the time, Pallas kernels for 0%

commit v1 on v0

v1 whole, which is shorter than its diff:
```python
import math

import jax
import jax.numpy as jnp
from jax import lax
from jax.sharding import PartitionSpec as P

F32 = jnp.float32
BF16 = jnp.bfloat16
AXES = ("row", "col")


def flat_pairs(target):
    pairs = []
    for row in range(8):
        for col in range(16):
            where = target(row // 4, row % 4, col // 4, (col // 2) % 2, col % 2)
            y_lo, z, x, y_hi, core = where
            pairs.append(
                (row * 16 + col, (y_lo * 4 + z % 4) * 16 + (x % 4) * 4 + y_hi * 2 + core)
            )
    return pairs


def core_swap(v):
    return lax.ppermute(v, AXES, flat_pairs(lambda yl, z, x, yh, c: (yl, z, x, yh, 1 - c)))


def y_hi_swap(v):
    return lax.ppermute(v, AXES, flat_pairs(lambda yl, z, x, yh, c: (yl, z, x, 1 - yh, c)))


def y_lo_swap(v):
    return lax.ppermute(v, AXES, flat_pairs(lambda yl, z, x, yh, c: (1 - yl, z, x, yh, c)))


def x_shift(v, step):
    return lax.ppermute(v, AXES, flat_pairs(lambda yl, z, x, yh, c: (yl, z, x + step, yh, c)))


def x_split_shift(v):
    return lax.ppermute(
        v, AXES, flat_pairs(lambda yl, z, x, yh, c: (yl, z, x + 1 - 2 * c, yh, c))
    )


def z_shift(v, step):
    return lax.ppermute(v, AXES, flat_pairs(lambda yl, z, x, yh, c: (yl, z + step, x, yh, c)))


def z_flip(v, mask):
    return lax.ppermute(v, AXES, flat_pairs(lambda yl, z, x, yh, c: (yl, z ^ mask, x, yh, c)))


def dot(a, b, ca, cb):
    return lax.dot_general(a, b, (((ca,), (cb,)), ((), ())), preferred_element_type=F32)


def gather_x(block, y_hi, core):
    beside = y_hi_swap(block)
    first = y_hi == 0
    here = jnp.concatenate(
        [jnp.where(first, block, beside), jnp.where(first, beside, block)], axis=1
    )
    below = x_shift(here, 1)
    above = x_shift(here, -1)
    across = x_split_shift(jnp.where(core == 0, below, above))
    return {0: here, -1: below, 1: above, 2: across}


def reduce_z(whole, z, y_lo):
    parts = whole.reshape(2, 4, 256, 512)

    def take(step):
        return lax.dynamic_index_in_dim(parts, (z + step) % 4, 1, keepdims=False)

    total = take(0).astype(F32)
    for step in (1, 3, 2):
        total = total + z_shift(take(step), step).astype(F32)
    mine = lax.dynamic_index_in_dim(total, y_lo, 0, keepdims=False)
    other = lax.dynamic_index_in_dim(total, 1 - y_lo, 0, keepdims=False)
    return mine + y_lo_swap(other.astype(BF16)).astype(F32)


def local(
    inputs,
    cotangent,
    conv_out,
    pre_act,
    weight_in,
    weight_out,
    scale_mid,
    scale_wide,
    keep_mid,
    keep_wide,
):
    rows, width = inputs.shape
    half = rows // 2
    scaling = 1.0 / math.sqrt(rows * lax.axis_size("row"))
    row, col = lax.axis_index("row"), lax.axis_index("col")
    y_lo, z = row // 4, row % 4
    x, y_hi, core = col // 4, (col // 2) % 2, col % 2

    def mine(v):
        return lax.dynamic_slice_in_dim(v, core * half, half, 0)

    def theirs(v):
        return lax.dynamic_slice_in_dim(v, (1 - core) * half, half, 0)

    out_full = lax.all_gather(weight_out, "row", axis=0, tiled=True)
    in_full = lax.all_gather(weight_in, "row", axis=1, tiled=True)

    wide_gain = scale_wide * keep_wide.astype(F32)
    cot_float = cotangent.astype(F32)
    grad_conv = (cot_float * wide_gain).astype(BF16)
    wide_part = jnp.sum(cot_float * conv_out.astype(F32), axis=0)
    conv_mine, conv_theirs = mine(grad_conv), theirs(grad_conv)
    conv_beside = core_swap(conv_theirs)

    gain_pair = jnp.stack([scale_mid, keep_mid.astype(F32)])
    gain_beside = core_swap(gain_pair)
    pre_mine = mine(pre_act)
    pre_beside = core_swap(theirs(pre_act))

    def chip_order(a, b):
        return jnp.concatenate(
            [jnp.where(core == 0, a, b), jnp.where(core == 0, b, a)], axis=1
        )

    pre_chip = chip_order(pre_mine, pre_beside).astype(F32)
    gain_chip = chip_order(gain_pair, gain_beside)
    mid_gain = gain_chip[0] * gain_chip[1]
    hidden = jnp.maximum(pre_chip * mid_gain, 0.0).astype(BF16)
    hid = gather_x(hidden, y_hi, core)

    out_beside = core_swap(out_full)

    def partial(step):
        at = ((x + step) % 4) * 512
        a = lax.dynamic_slice_in_dim(out_full, at, 512, 0)
        b = lax.dynamic_slice_in_dim(out_beside, at, 512, 0)
        return dot(conv_mine, a, 1, 1) + dot(conv_beside, b, 1, 1)

    sends = {step: x_shift(partial(step).astype(BF16), step) for step in (2, 1, 3)}
    total = partial(0)
    for step in (1, 3, 2):
        total = total + sends[step].astype(F32)
    total = total.reshape(half, 2, 256)
    own = lax.dynamic_index_in_dim(total, y_hi, 1, keepdims=False)
    away = lax.dynamic_index_in_dim(total, 1 - y_hi, 1, keepdims=False)
    grad_hid = own + y_hi_swap(away.astype(BF16)).astype(F32)
    alive = (pre_chip > 0) & (gain_chip[1] > 0)[None, :]
    grad_pre = jnp.where(alive, grad_hid, 0.0)
    mid_part = jnp.sum(grad_pre * pre_chip, axis=0).reshape(2, 128)
    grad_act = (grad_pre * mid_gain).astype(BF16)
    act = gather_x(grad_act, y_hi, core)

    mid_own = lax.dynamic_index_in_dim(mid_part, core, 0, keepdims=False)
    mid_away = lax.dynamic_index_in_dim(mid_part, 1 - core, 0, keepdims=False)
    mid_own = mid_own + core_swap(mid_away)
    sums = jnp.concatenate([mid_own, wide_part]).reshape(5, 128)
    sums = sums + z_flip(sums, 1)
    sums = sums + z_flip(sums, 2)
    sums = sums + y_lo_swap(sums)
    grad_smid = keep_mid.astype(F32) * scaling * sums[0]
    grad_swide = keep_wide.astype(F32) * scaling * sums[1:].reshape(512)

    def weight_partial(blocks, a_mine, a_theirs):
        whole = jnp.zeros((2048, 512), BF16)
        for step, block in blocks.items():
            product = dot(block, a_mine, 0, 0) + dot(core_swap(block), a_theirs, 0, 0)
            whole = lax.dynamic_update_slice_in_dim(
                whole, product.astype(BF16), ((x + step) % 4) * 512, 0
            )
        return whole

    wout = weight_partial(hid, conv_mine, conv_theirs)
    grad_wout = (
        lax.psum_scatter(wout, "row", scatter_dimension=0, tiled=True).astype(F32) * scaling
    )

    act_beside = {step: core_swap(block) for step, block in act.items()}
    win = jnp.zeros((2048, 512), BF16)
    in_mine, in_theirs = mine(inputs), theirs(inputs)
    grad_mine, grad_theirs = mine(cotangent).astype(F32), theirs(cotangent).astype(F32)
    for step, block in act.items():
        at = ((x + step) % 4) * 512
        product = dot(block, in_mine, 0, 0) + dot(act_beside[step], in_theirs, 0, 0)
        win = lax.dynamic_update_slice_in_dim(win, product.astype(BF16), at, 0)
        weights = lax.dynamic_slice_in_dim(in_full, at, 512, 1)
        grad_mine = grad_mine + dot(block, weights, 1, 1)
        grad_theirs = grad_theirs + dot(act_beside[step], weights, 1, 1)
    grad_win = (reduce_z(win, z, y_lo) * scaling).T
    grad_x = jnp.zeros((rows, width), BF16)
    grad_x = lax.dynamic_update_slice_in_dim(grad_x, grad_mine.astype(BF16), core * half, 0)
    grad_x = lax.dynamic_update_slice_in_dim(
        grad_x, grad_theirs.astype(BF16), (1 - core) * half, 0
    )
    return (grad_x, grad_win, grad_wout, grad_smid, grad_swide)


def solution(mesh):
    return jax.shard_map(
        local,
        mesh=mesh,
        in_specs=(
            P("row", "col"),
            P("row", "col"),
            P("row", "col"),
            P("row", "col"),
            P("col", "row"),
            P("row", "col"),
            P("col"),
            P("col"),
            P("col"),
            P("col"),
        ),
        out_specs=(P("row", "col"), P("col", "row"), P("row", "col"), P("col"), P("col")),
        check_vma=False,
    )
```

time: 446 us -> 289 us (0.65)
  waiting for transfers between devices: 360 us -> 148 us
  starting transfers between devices: 0.28 us -> 30.2 us
  matrix products: 31.9 us -> 57.4 us
  blocking collectives: 19.1 us -> 0 us
  other arithmetic: 7.77 us -> 22.9 us
    all_gather x4 -> x2, waiting for transfers between devices: 190 us -> 46.1 us  [the longest x1 46.1 us: local(): out_full = lax.all_gather(weight_out, 'row', axis=0, tiled=True)]
    ppermute x0 -> x32, waiting for transfers between devices: none -> 101 us  [the longest x7 46 us: x_shift(): lax.ppermute(v, AXES, flat_pairs(lambda yl, z, x, yh, c: (yl, z, x + step...]
    unnamed x8 -> x3, waiting for transfers between devices: 89.9 us -> 0.71 us
    reduce_scatter x2 -> x1, waiting for transfers between devices: 79.6 us -> 0.01 us  [local(): lax.psum_scatter(wout, 'row', scatter_dimension=0, tiled=True).astype(F32)]
    ppermute x0 -> x32, starting transfers between devices: none -> 30.1 us  [the longest x7 12.3 us: x_shift(): lax.ppermute(v, AXES, flat_pairs(lambda yl, z, x, yh, c: (yl, z, x + step...]
    dot_general x4 -> x32, matrix products: 31.9 us -> 57.4 us  [dot(): lax.dot_general(a, b, (((ca,), (cb,)), ((), ())), preferred_element_type=...]
    psum x1 -> x0, blocking collectives: 19.1 us -> none  [local(): mid_sum, wide_sum = lax.psum((mid_part, wide_part), 'row')]
    select_n x0 -> x6, other arithmetic: none -> 7.43 us  [the longest x2 3.34 us: gather_x(): across = x_split_shift(jnp.where(core == 0, below, above))]
  transfers between devices with their start and end apart: 7 -> 35, of which waited for: 7 -> 17; matrix products, arithmetic and copies ran while one was open for 7% -> 31% of each run, Pallas kernels for 0% -> 0%
where the time goes in v1:
time: 289 us; the launch traced here: 287 us
  waiting for transfers between devices  148 us (51%)
  matrix products  57.4 us (20%)
  starting transfers between devices  30.2 us (10%)
  other arithmetic  22.9 us (8%)
  local copies, waits for them, and re-layouts  14.6 us (5%)
  between operations  14.3 us (5%)
    dot_general x32, matrix products, dot(): lax.dot_general(a, b, (((ca,), (cb,)), ((), ())), preferred_element_type=...  57.4 us
    all_gather x1, waiting for transfers between devices, local(): out_full = lax.all_gather(weight_out, 'row', axis=0, tiled=True)  46.1 us
    ppermute x7, waiting for transfers between devices, x_shift(): lax.ppermute(v, AXES, flat_pairs(lambda yl, z, x, yh, c: (yl, z, x + step...  46 us
    ppermute x3, waiting for transfers between devices, z_shift(): lax.ppermute(v, AXES, flat_pairs(lambda yl, z, x, yh, c: (yl, z + step, x...  32.8 us
    ppermute x7, starting transfers between devices, x_shift(): lax.ppermute(v, AXES, flat_pairs(lambda yl, z, x, yh, c: (yl, z, x + step...  12.3 us
    ppermute x3, waiting for transfers between devices, y_hi_swap(): lax.ppermute(v, AXES, flat_pairs(lambda yl, z, x, yh, c: (yl, z, x, 1 - y...  8.01 us
    ppermute x3, starting transfers between devices, y_hi_swap(): lax.ppermute(v, AXES, flat_pairs(lambda yl, z, x, yh, c: (yl, z, x, 1 - y...  7.22 us
    ppermute x2, waiting for transfers between devices, z_flip(): lax.ppermute(v, AXES, flat_pairs(lambda yl, z, x, yh, c: (yl, z ^ mask, x...  6.78 us
  transfers between devices with their start and end apart: 35, of which 17 were waited for; matrix products, arithmetic and copies ran while one was open for 31% of the time, Pallas kernels for 0%

profile of v1, /device:TPU:0, one launch (start us, length us, event | category | flops | bytes accessed | tf_op | source)
XLA Modules:
  0.0 287.3 jit_solution(2326742918318241632)
XLA Ops:
  8.0 46.1 %all-gather.3.cloned.1.call-done = bf16[2048,512]{1,0:T(8,128)(2,1)} async-done(((bf16[256,512]{1,0:T(8,128)(2,1)}), bf16[2048,512]{1,0:T(8,128)(2,1)}) %all-gather.3.cloned.1.call-update) | async-done | bytes 2097168 | tf_op jit(solution)/shard_map/all_gather | solution.py:110
  54.8 2.6 fusion.1
  62.7 2.8 add_convert_fusion.4
  66.9 2.8 add_convert_fusion.3
  71.5 2.8 add_convert_fusion.2
  81.9 4.9 %collective-permute-done.4 = bf16[768,512]{0,1:T(8,128)(2,1)} collective-permute-done((bf16[768,512]{0,1:T(8,128)(2,1)}, bf16[768,512]{0,1:T(8,128)(2,1)}, u32[]{:S(2)}, u32[]{:S(2)}) %collective-permute-start.4) | collective-permute-done | bytes 786464 | tf_op jit(solution)/shard_map/ppermute | solution.py:38
  86.8 19.0 %collective-permute-done.5 = bf16[768,512]{0,1:T(8,128)(2,1)} collective-permute-done((bf16[768,512]{0,1:T(8,128)(2,1)}, bf16[768,512]{0,1:T(8,128)(2,1)}, u32[]{:S(2)}, u32[]{:S(2)}) %collective-permute-start.5) | collective-permute-done | bytes 786464 | tf_op jit(solution)/shard_map/ppermute | solution.py:38
  105.8 2.0 convert_add_fusion
  109.9 2.7 collective-permute-start.7
  115.2 2.1 constant_dynamic-slice_fusion.3
  117.3 2.3 copy.30
  119.6 5.7 %collective-permute-done.7 = bf16[768,256]{1,0:T(8,128)(2,1)S(1)} collective-permute-done((bf16[768,256]{1,0:T(8,128)(2,1)}, bf16[768,256]{1,0:T(8,128)(2,1)S(1)}, u32[]{:S(2)}, u32[]{:S(2)}) %collective-permute-start.7) | collective-permute-done | bytes 393248 | tf_op jit(solution)/shard_map/ppermute | solution.py:30
  126.0 2.5 fusion.22
  131.4 2.0 collective-permute-done.29
  133.8 4.8 %collective-permute-done.30 = f32[5,128]{1,0:T(8,128)} collective-permute-done((f32[5,128]{1,0:T(8,128)S(1)}, f32[5,128]{1,0:T(8,128)}, u32[]{:S(2)}, u32[]{:S(2)}) %collective-permute-start.30) | collective-permute-done | bytes 2592 | tf_op jit(solution)/shard_map/ppermute | solution.py:52
  139.9 2.9 %collective-permute-start.8 = (bf16[768,256]{1,0:T(8,128)(2,1)S(1)}, bf16[768,256]{1,0:T(8,128)(2,1)S(1)}, u32[]{:S(2)}, u32[]{:S(2)}) collective-permute-start(bf16[768,256]{1,0:T(8,128)(2,1)S(1)} %get-tuple-element.21), channel_id=1, source_target_pairs={{0,2},{1,3},{2,0},{3,1},{4,6},{5,7},{6,4},{7,5},{8,10},{9,11},{10,... | collective-permute-start | bytes 1179656 | tf_op jit(solution)/shard_map/ppermute | solution.py:30
  145.9 2.4 collective-permute-start.22
  154.1 2.4 collective-permute-start.9
  158.9 3.0 %fusion.72 = f32[768,512]{1,0:T(8,128)} fusion(bf16[512,2048]{1,0:T(8,128)(2,1)} %all-gather.5.cloned.1.call-done, s32[]{:T(128)S(6)} %select_n.227, bf16[768,256]{1,0:T(8,128)(2,1)} %copy-done.8, bf16[768,256]{1,0:T(8,128)(2,1)S(1)} %get-tuple-element.26), kind=kOutput, calls=%fused_computation.100 | convolution fusion | flops 404226048 | bytes 2883588 | tf_op jit(solution)/shard_map/dot_general | solution.py:56
  161.8 6.4 %collective-permute-done.22 = bf16[768,512]{1,0:T(8,128)(2,1)} collective-permute-done((bf16[768,512]{1,0:T(8,128)(2,1)}, bf16[768,512]{1,0:T(8,128)(2,1)}, u32[]{:S(2)}, u32[]{:S(2)}) %collective-permute-start.22) | collective-permute-done | bytes 786464 | tf_op jit(solution)/shard_map/ppermute | solution.py:38
  171.0 12.0 %collective-permute-done.9 = bf16[768,512]{1,0:T(8,128)(2,1)} collective-permute-done((bf16[768,512]{1,0:T(8,128)(2,1)}, bf16[768,512]{1,0:T(8,128)(2,1)}, u32[]{:S(2)}, u32[]{:S(2)}) %collective-permute-start.9) | collective-permute-done | bytes 786464 | tf_op jit(solution)/shard_map/ppermute | solution.py:38
  183.0 2.9 %collective-permute-done.10 = bf16[768,512]{1,0:T(8,128)(2,1)} collective-permute-done((bf16[768,512]{1,0:T(8,128)(2,1)}, bf16[768,512]{1,0:T(8,128)(2,1)}, u32[]{:S(2)}, u32[]{:S(2)}) %collective-permute-start.10) | collective-permute-done | bytes 786464 | tf_op jit(solution)/shard_map/ppermute | solution.py:38
  185.9 2.1 broadcast_select_fusion.1
  192.3 2.9 %fusion.64 = f32[768,512]{1,0:T(8,128)} fusion(bf16[768,512]{1,0:T(8,128)(2,1)} %collective-permute-done.10, bf16[512,2048]{1,0:T(8,128)(2,1)S(1)} %copy-done.1, s32[]{:T(128)S(6)} %select_n.229), kind=kOutput, calls=%fused_computation.92 | convolution fusion | flops 402653184 | bytes 2883588 | tf_op jit(solution)/shard_map/dot_general | solution.py:56
  197.7 2.8 fusion.51
  203.4 2.9 %fusion.68 = f32[768,512]{1,0:T(8,128)} fusion(bf16[768,512]{1,0:T(8,128)(2,1)} %collective-permute-done.9, bf16[512,2048]{1,0:T(8,128)(2,1)S(1)} %copy-done.1, s32[]{:T(128)S(6)} %select_n.240), kind=kOutput, calls=%fused_computation.96 | convolution fusion | flops 402653184 | bytes 2883588 | tf_op jit(solution)/shard_map/dot_general | solution.py:56
  206.9 2.6 fusion.12
  209.4 2.6 fusion.11
  212.6 2.6 fusion.10
  228.7 2.0 collective-permute-start.16
  236.7 32.8 %collective-permute-done.16 = bf16[2,256,512]{2,1,0:T(8,128)(2,1)S(1)} collective-permute-done((bf16[2,256,512]{2,1,0:T(8,128)(2,1)S(1)}, bf16[2,256,512]{2,1,0:T(8,128)(2,1)S(1)}, u32[]{:S(2)}, u32[]{:S(2)}) %collective-permute-start.16) | collective-permute-done | bytes 524320 | tf_op jit(solution)/shard_map/ppermute | solution.py:48
  272.8 5.0 %collective-permute-done.19 = bf16[256,512]{1,0:T(8,128)(2,1)S(1)} collective-permute-done((bf16[256,512]{1,0:T(8,128)(2,1)S(1)}, bf16[256,512]{1,0:T(8,128)(2,1)S(1)}, u32[]{:S(2)}, u32[]{:S(2)}) %collective-permute-start.19) | collective-permute-done | bytes 262176 | tf_op jit(solution)/shard_map/ppermute | solution.py:34
  (162 shorter events, 77.8 us)
Async XLA Ops:
  7.2 46.9 %all-gather.3.cloned.1.call-start = ((), (), s32[]{:S(2)}) async-start(), calls=%async_computation.1 | async-start | bytes 2359296 | tf_op jit(solution)/shard_map/all_gather | solution.py:110
  7.9 150.9 %all-gather.5.cloned.1.call-start = ((), (), s32[]{:S(2)}) async-start(), calls=%async_computation.2 | async-start | bytes 2359296 | tf_op jit(solution)/shard_map/all_gather | solution.py:111
  54.1 8.6 %collective-permute-start.3 = (bf16[2048,512]{1,0:T(8,128)(2,1)}, bf16[2048,512]{1,0:T(8,128)(2,1)}, u32[]{:S(2)}, u32[]{:S(2)}) collective-permute-start(bf16[2048,512]{1,0:T(8,128)(2,1)} %all-gather.3.cloned.1.call-done), channel_id=1, source_target_pairs={{0,1},{1,0},{2,3},{3,2},{4,5},{5,4},{6,7},{7,6},{8,9},{9,8},{10,11... | collective-permute-start | bytes 6291464 | tf_op jit(solution)/shard_map/ppermute | solution.py:26
  58.3 4.4 %collective-permute-start.2 = (bf16[768,512]{1,0:T(8,128)(2,1)}, bf16[768,512]{1,0:T(8,128)(2,1)}, u32[]{:S(2)}, u32[]{:S(2)}) collective-permute-start(bf16[768,512]{1,0:T(8,128)(2,1)} %constant_dynamic-slice_fusion.4), channel_id=1, source_target_pairs={{0,1},{1,0},{2,3},{3,2},{4,5},{5,4},{6,7},{7,6},{8,9},{9,8},{10,11... | collective-permute-start | bytes 2359304 | tf_op jit(solution)/shard_map/ppermute | solution.py:26
  59.5 53.9 %collective-permute-start = (bf16[768,128]{1,0:T(8,128)(2,1)}, bf16[768,128]{1,0:T(8,128)(2,1)}, u32[]{:S(2)}, u32[]{:S(2)}) collective-permute-start(bf16[768,128]{1,0:T(8,128)(2,1)} %constant_dynamic-slice_fusion.5), channel_id=1, source_target_pairs={{0,1},{1,0},{2,3},{3,2},{4,5},{5,4},{6,7},{7,6},{8,9},{9,8},{10,11... | collective-permute-start | bytes 589832 | tf_op jit(solution)/shard_map/ppermute | solution.py:26
  65.4 21.4 %collective-permute-start.4 = (bf16[768,512]{0,1:T(8,128)(2,1)}, bf16[768,512]{0,1:T(8,128)(2,1)}, u32[]{:S(2)}, u32[]{:S(2)}) collective-permute-start(bf16[768,512]{0,1:T(8,128)(2,1)} %add_convert_fusion.4), channel_id=1, source_target_pairs={{0,4},{1,5},{2,6},{3,7},{4,8},{5,9},{6,10},{7,11},{8,12},{9,13},{1... | collective-permute-start | bytes 2359304 | tf_op jit(solution)/shard_map/ppermute | solution.py:38
  69.7 36.1 %collective-permute-start.5 = (bf16[768,512]{0,1:T(8,128)(2,1)}, bf16[768,512]{0,1:T(8,128)(2,1)}, u32[]{:S(2)}, u32[]{:S(2)}) collective-permute-start(bf16[768,512]{0,1:T(8,128)(2,1)} %add_convert_fusion.3), channel_id=1, source_target_pairs={{0,12},{1,13},{2,14},{3,15},{4,0},{5,1},{6,2},{7,3},{8,4},{9,5},{1... | collective-permute-start | bytes 2359304 | tf_op jit(solution)/shard_map/ppermute | solution.py:38
  74.3 31.5 %collective-permute-start.6 = (bf16[768,512]{0,1:T(8,128)(2,1)}, bf16[768,512]{0,1:T(8,128)(2,1)}, u32[]{:S(2)}, u32[]{:S(2)}) collective-permute-start(bf16[768,512]{0,1:T(8,128)(2,1)} %add_convert_fusion.2), channel_id=1, source_target_pairs={{0,8},{1,9},{2,10},{3,11},{4,12},{5,13},{6,14},{7,15},{8,0},{9,1},... | collective-permute-start | bytes 2359304 | tf_op jit(solution)/shard_map/ppermute | solution.py:38
  76.2 202.8 %reduce-scatter.2.cloned.1.call-start = ((), (), s32[]{:S(2)}) async-start(), calls=%async_computation.3 | async-start | bytes 2359296 | tf_op jit(solution)/shard_map/reduce_scatter | solution.py:179
  109.9 15.3 %collective-permute-start.7 = (bf16[768,256]{1,0:T(8,128)(2,1)}, bf16[768,256]{1,0:T(8,128)(2,1)S(1)}, u32[]{:S(2)}, u32[]{:S(2)}) collective-permute-start(bf16[768,256]{1,0:T(8,128)(2,1)} %bitcast.86), channel_id=1, source_target_pairs={{0,2},{1,3},{2,0},{3,1},{4,6},{5,7},{6,4},{7,5},{8,10},{9,11},{10,... | collective-permute-start | bytes 1179656 | tf_op jit(solution)/shard_map/ppermute | solution.py:30
  129.8 13.9 %collective-permute-start.20 = (bf16[768,256]{1,0:T(8,128)(2,1)}, bf16[768,256]{1,0:T(8,128)(2,1)}, u32[]{:S(2)}, u32[]{:S(2)}) collective-permute-start(bf16[768,256]{1,0:T(8,128)(2,1)} %get-tuple-element.30), channel_id=1, source_target_pairs={{0,2},{1,3},{2,0},{3,1},{4,6},{5,7},{6,4},{7,5},{8,10},{9,11},{10,... | collective-permute-start | bytes 1179656 | tf_op jit(solution)/shard_map/ppermute | solution.py:30
  133.4 5.2 %collective-permute-start.30 = (f32[5,128]{1,0:T(8,128)S(1)}, f32[5,128]{1,0:T(8,128)}, u32[]{:S(2)}, u32[]{:S(2)}) collective-permute-start(f32[5,128]{1,0:T(8,128)S(1)} %fusion.119), channel_id=1, source_target_pairs={{0,32},{1,33},{2,34},{3,35},{4,36},{5,37},{6,38},{7,39},{8,40},{9,... | collective-permute-start | bytes 7688 | tf_op jit(solution)/shard_map/ppermute | solution.py:52
  139.3 3.8 %collective-permute-start.31 = (f32[5,128]{1,0:T(8,128)S(1)}, f32[5,128]{1,0:T(8,128)S(1)}, u32[]{:S(2)}, u32[]{:S(2)}) collective-permute-start(f32[5,128]{1,0:T(8,128)S(1)} %fusion.151), channel_id=1, source_target_pairs={{0,64},{1,65},{2,66},{3,67},{4,68},{5,69},{6,70},{7,71},{8,72},{9,... | collective-permute-start | bytes 7688 | tf_op jit(solution)/shard_map/ppermute | solution.py:34
  139.9 11.4 %collective-permute-start.8 = (bf16[768,256]{1,0:T(8,128)(2,1)S(1)}, bf16[768,256]{1,0:T(8,128)(2,1)S(1)}, u32[]{:S(2)}, u32[]{:S(2)}) collective-permute-start(bf16[768,256]{1,0:T(8,128)(2,1)S(1)} %get-tuple-element.21), channel_id=1, source_target_pairs={{0,2},{1,3},{2,0},{3,1},{4,6},{5,7},{6,4},{7,5},{8,10},{9,11},{10,... | collective-permute-start | bytes 1179656 | tf_op jit(solution)/shard_map/ppermute | solution.py:30
  145.9 22.4 %collective-permute-start.22 = (bf16[768,512]{1,0:T(8,128)(2,1)}, bf16[768,512]{1,0:T(8,128)(2,1)}, u32[]{:S(2)}, u32[]{:S(2)}) collective-permute-start(bf16[768,512]{1,0:T(8,128)(2,1)} %pad_maximum_fusion.1), channel_id=1, source_target_pairs={{0,4},{1,5},{2,6},{3,7},{4,8},{5,9},{6,10},{7,11},{8,12},{9,13},{1... | collective-permute-start | bytes 2359304 | tf_op jit(solution)/shard_map/ppermute | solution.py:38
  148.3 20.8 %collective-permute-start.24 = (bf16[768,512]{1,0:T(8,128)(2,1)}, bf16[768,512]{1,0:T(8,128)(2,1)}, u32[]{:S(2)}, u32[]{:S(2)}) collective-permute-start(bf16[768,512]{1,0:T(8,128)(2,1)} %pad_maximum_fusion.1), channel_id=1, source_target_pairs={{0,12},{1,13},{2,14},{3,15},{4,0},{5,1},{6,2},{7,3},{8,4},{9,5},{1... | collective-permute-start | bytes 2359304 | tf_op jit(solution)/shard_map/ppermute | solution.py:38
  154.1 28.9 %collective-permute-start.9 = (bf16[768,512]{1,0:T(8,128)(2,1)}, bf16[768,512]{1,0:T(8,128)(2,1)}, u32[]{:S(2)}, u32[]{:S(2)}) collective-permute-start(bf16[768,512]{1,0:T(8,128)(2,1)} %pad_maximum_fusion), channel_id=1, source_target_pairs={{0,4},{1,5},{2,6},{3,7},{4,8},{5,9},{6,10},{7,11},{8,12},{9,13},{1... | collective-permute-start | bytes 2359304 | tf_op jit(solution)/shard_map/ppermute | solution.py:38
  156.5 29.4 %collective-permute-start.10 = (bf16[768,512]{1,0:T(8,128)(2,1)}, bf16[768,512]{1,0:T(8,128)(2,1)}, u32[]{:S(2)}, u32[]{:S(2)}) collective-permute-start(bf16[768,512]{1,0:T(8,128)(2,1)} %pad_maximum_fusion), channel_id=1, source_target_pairs={{0,12},{1,13},{2,14},{3,15},{4,0},{5,1},{6,2},{7,3},{8,4},{9,5},{1... | collective-permute-start | bytes 2359304 | tf_op jit(solution)/shard_map/ppermute | solution.py:38
  158.9 36.4 %collective-permute-start.21 = (bf16[768,512]{1,0:T(8,128)(2,1)}, bf16[768,512]{1,0:T(8,128)(2,1)}, u32[]{:S(2)}, u32[]{:S(2)}) collective-permute-start(bf16[768,512]{1,0:T(8,128)(2,1)} %pad_maximum_fusion.1), channel_id=1, source_target_pairs={{0,1},{1,0},{2,3},{3,2},{4,5},{5,4},{6,7},{7,6},{8,9},{9,8},{10,11... | collective-permute-start | bytes 2359304 | tf_op jit(solution)/shard_map/ppermute | solution.py:26
  168.3 48.8 %collective-permute-start.12 = (bf16[768,512]{1,0:T(8,128)(2,1)}, bf16[768,512]{1,0:T(8,128)(2,1)}, u32[]{:S(2)}, u32[]{:S(2)}) collective-permute-start(bf16[768,512]{1,0:T(8,128)(2,1)} %pad_maximum_fusion), channel_id=1, source_target_pairs={{0,1},{1,0},{2,3},{3,2},{4,5},{5,4},{6,7},{7,6},{8,9},{9,8},{10,11... | collective-permute-start | bytes 2359304 | tf_op jit(solution)/shard_map/ppermute | solution.py:26
  170.3 36.0 %collective-permute-start.26 = (bf16[768,512]{1,0:T(8,128)(2,1)S(1)}, bf16[768,512]{1,0:T(8,128)(2,1)S(1)}, u32[]{:S(2)}, u32[]{:S(2)}) collective-permute-start(bf16[768,512]{1,0:T(8,128)(2,1)S(1)} %broadcast_select_fusion), channel_id=1, source_target_pairs={{0,4},{1,13},{2,6},{3,15},{4,8},{5,1},{6,10},{7,3},{8,12},{9,5},{1... | collective-permute-start | bytes 2359304 | tf_op jit(solution)/shard_map/ppermute | solution.py:42
  188.0 34.3 %collective-permute-start.11 = (bf16[768,512]{1,0:T(8,128)(2,1)}, bf16[768,512]{1,0:T(8,128)(2,1)}, u32[]{:S(2)}, u32[]{:S(2)}) collective-permute-start(bf16[768,512]{1,0:T(8,128)(2,1)} %broadcast_select_fusion.1), channel_id=1, source_target_pairs={{0,4},{1,13},{2,6},{3,15},{4,8},{5,1},{6,10},{7,3},{8,12},{9,5},{1... | collective-permute-start | bytes 2359304 | tf_op jit(solution)/shard_map/ppermute | solution.py:42
  188.7 17.7 %collective-permute-start.23 = (bf16[768,512]{1,0:T(8,128)(2,1)}, bf16[768,512]{1,0:T(8,128)(2,1)S(1)}, u32[]{:S(2)}, u32[]{:S(2)}) collective-permute-start(bf16[768,512]{1,0:T(8,128)(2,1)} %collective-permute-done.22), channel_id=1, source_target_pairs={{0,1},{1,0},{2,3},{3,2},{4,5},{5,4},{6,7},{7,6},{8,9},{9,8},{10,11... | collective-permute-start | bytes 2359304 | tf_op jit(solution)/shard_map/ppermute | solution.py:26
  195.2 14.2 %collective-permute-start.25 = (bf16[768,512]{1,0:T(8,128)(2,1)}, bf16[768,512]{1,0:T(8,128)(2,1)S(1)}, u32[]{:S(2)}, u32[]{:S(2)}) collective-permute-start(bf16[768,512]{1,0:T(8,128)(2,1)} %collective-permute-done.24), channel_id=1, source_target_pairs={{0,1},{1,0},{2,3},{3,2},{4,5},{5,4},{6,7},{7,6},{8,9},{9,8},{10,11... | collective-permute-start | bytes 2359304 | tf_op jit(solution)/shard_map/ppermute | solution.py:26
  206.3 19.1 %collective-permute-start.13 = (bf16[768,512]{1,0:T(8,128)(2,1)}, bf16[768,512]{1,0:T(8,128)(2,1)}, u32[]{:S(2)}, u32[]{:S(2)}) collective-permute-start(bf16[768,512]{1,0:T(8,128)(2,1)} %collective-permute-done.9), channel_id=1, source_target_pairs={{0,1},{1,0},{2,3},{3,2},{4,5},{5,4},{6,7},{7,6},{8,9},{9,8},{10,11... | collective-permute-start | bytes 2359304 | tf_op jit(solution)/shard_map/ppermute | solution.py:26
  206.4 6.2 %collective-permute-start.27 = (bf16[768,512]{1,0:T(8,128)(2,1)S(1)}, bf16[768,512]{1,0:T(8,128)(2,1)S(1)}, u32[]{:S(2)}, u32[]{:S(2)}) collective-permute-start(bf16[768,512]{1,0:T(8,128)(2,1)S(1)} %collective-permute-done.26), channel_id=1, source_target_pairs={{0,1},{1,0},{2,3},{3,2},{4,5},{5,4},{6,7},{7,6},{8,9},{9,8},{10,11... | collective-permute-start | bytes 2359304 | tf_op jit(solution)/shard_map/ppermute | solution.py:26
  216.9 6.1 %collective-permute-start.14 = (bf16[768,512]{1,0:T(8,128)(2,1)}, bf16[768,512]{1,0:T(8,128)(2,1)S(1)}, u32[]{:S(2)}, u32[]{:S(2)}) collective-permute-start(bf16[768,512]{1,0:T(8,128)(2,1)} %collective-permute-done.10), channel_id=1, source_target_pairs={{0,1},{1,0},{2,3},{3,2},{4,5},{5,4},{6,7},{7,6},{8,9},{9,8},{10,11... | collective-permute-start | bytes 2359304 | tf_op jit(solution)/shard_map/ppermute | solution.py:26
  222.3 5.5 %collective-permute-start.15 = (bf16[768,512]{1,0:T(8,128)(2,1)}, bf16[768,512]{1,0:T(8,128)(2,1)S(1)}, u32[]{:S(2)}, u32[]{:S(2)}) collective-permute-start(bf16[768,512]{1,0:T(8,128)(2,1)} %collective-permute-done.11), channel_id=1, source_target_pairs={{0,1},{1,0},{2,3},{3,2},{4,5},{5,4},{6,7},{7,6},{8,9},{9,8},{10,11... | collective-permute-start | bytes 2359304 | tf_op jit(solution)/shard_map/ppermute | solution.py:26
  228.7 40.8 %collective-permute-start.16 = (bf16[2,256,512]{2,1,0:T(8,128)(2,1)S(1)}, bf16[2,256,512]{2,1,0:T(8,128)(2,1)S(1)}, u32[]{:S(2)}, u32[]{:S(2)}) collective-permute-start(bf16[2,256,512]{2,1,0:T(8,128)(2,1)S(1)} %get-tuple-element.17), channel_id=1, source_target_pairs={{0,16},{1,17},{2,18},{3,19},{4,20},{5,21},{6,22},{7,23},{8,24},{9,... | collective-permute-start | bytes 1572872 | tf_op jit(solution)/shard_map/ppermute | solution.py:48
  230.7 38.8 %collective-permute-start.17 = (bf16[2,256,512]{2,1,0:T(8,128)(2,1)S(1)}, bf16[2,256,512]{2,1,0:T(8,128)(2,1)S(1)}, u32[]{:S(2)}, u32[]{:S(2)}) collective-permute-start(bf16[2,256,512]{2,1,0:T(8,128)(2,1)S(1)} %get-tuple-element.19), channel_id=1, source_target_pairs={{0,48},{1,49},{2,50},{3,51},{4,52},{5,53},{6,54},{7,55},{8,56},{9,... | collective-permute-start | bytes 1572872 | tf_op jit(solution)/shard_map/ppermute | solution.py:48
  232.0 37.5 %collective-permute-start.18 = (bf16[2,256,512]{2,1,0:T(8,128)(2,1)S(1)}, bf16[2,256,512]{2,1,0:T(8,128)(2,1)S(1)}, u32[]{:S(2)}, u32[]{:S(2)}) collective-permute-start(bf16[2,256,512]{2,1,0:T(8,128)(2,1)S(1)} %get-tuple-element.18), channel_id=1, source_target_pairs={{0,32},{1,33},{2,34},{3,35},{4,36},{5,37},{6,38},{7,39},{8,40},{9,... | collective-permute-start | bytes 1572872 | tf_op jit(solution)/shard_map/ppermute | solution.py:48
  269.8 8.0 %collective-permute-start.19 = (bf16[256,512]{1,0:T(8,128)(2,1)S(1)}, bf16[256,512]{1,0:T(8,128)(2,1)S(1)}, u32[]{:S(2)}, u32[]{:S(2)}) collective-permute-start(bf16[256,512]{1,0:T(8,128)(2,1)S(1)} %fusion.74), channel_id=1, source_target_pairs={{0,64},{1,65},{2,66},{3,67},{4,68},{5,69},{6,70},{7,71},{8,72},{9,... | collective-permute-start | bytes 786440 | tf_op jit(solution)/shard_map/ppermute | solution.py:34
  (28 other events, 305.3 us)
Sparse Core Ops, SparseCore 0:
  9.7 44.3 all-gather.2
  76.3 45.8 all-gather.4
  215.3 47.7 reduce-scatter.1

commit v2 on v1

--- a/solution.py
+++ b/solution.py
@@ -56,15 +56,25 @@
     return lax.dot_general(a, b, (((ca,), (cb,)), ((), ())), preferred_element_type=F32)
 
 
-def gather_x(block, y_hi, core):
-    beside = y_hi_swap(block)
-    first = y_hi == 0
-    here = jnp.concatenate(
-        [jnp.where(first, block, beside), jnp.where(first, beside, block)], axis=1
-    )
+def gather_x(block, core):
+    here = jnp.concatenate([block, y_hi_swap(block)], axis=1)
     below = x_shift(here, 1)
     above = x_shift(here, -1)
     across = x_split_shift(jnp.where(core == 0, below, above))
+    return {0: here, -1: below, 1: above, 2: across}
+
+
+def z_split_shift(v):
+    return lax.ppermute(
+        v, AXES, flat_pairs(lambda yl, z, x, yh, c: (yl, z + 1 - 2 * c, x, yh, c))
+    )
+
+
+def gather_z(block, core):
+    here = jnp.stack([block, y_lo_swap(block)])
+    below = z_shift(here, 1)
+    above = z_shift(here, -1)
+    across = z_split_shift(jnp.where(core == 0, below, above))
     return {0: here, -1: below, 1: above, 2: across}
 
 
@@ -107,8 +117,7 @@
     def theirs(v):
         return lax.dynamic_slice_in_dim(v, (1 - core) * half, half, 0)
 
-    out_full = lax.all_gather(weight_out, "row", axis=0, tiled=True)
-    in_full = lax.all_gather(weight_in, "row", axis=1, tiled=True)
+    out_blocks = gather_z(weight_out, core)
 
     wide_gain = scale_wide * keep_wide.astype(F32)
     cot_float = cotangent.astype(F32)
@@ -131,15 +140,23 @@
     gain_chip = chip_order(gain_pair, gain_beside)
     mid_gain = gain_chip[0] * gain_chip[1]
     hidden = jnp.maximum(pre_chip * mid_gain, 0.0).astype(BF16)
-    hid = gather_x(hidden, y_hi, core)
-
-    out_beside = core_swap(out_full)
+    hid = gather_x(hidden, core)
+
+    out_full = jnp.zeros((2, 4, 256, 1024), BF16)
+    for step, block in out_blocks.items():
+        wide = jnp.concatenate([block, core_swap(block)], axis=2)
+        for i, at in ((0, y_lo), (1, 1 - y_lo)):
+            out_full = lax.dynamic_update_slice(
+                out_full, wide[i][None, None], (at, (z + step) % 4, 0, 0)
+            )
+    out_full = out_full.reshape(2048, 1024)
+    conv_both = jnp.concatenate([conv_mine, conv_beside], axis=1)
+    weight_in, out_full = lax.optimization_barrier((weight_in, out_full))
+    in_full = lax.all_gather(weight_in, "row", axis=1, tiled=True)
 
     def partial(step):
         at = ((x + step) % 4) * 512
-        a = lax.dynamic_slice_in_dim(out_full, at, 512, 0)
-        b = lax.dynamic_slice_in_dim(out_beside, at, 512, 0)
-        return dot(conv_mine, a, 1, 1) + dot(conv_beside, b, 1, 1)
+        return dot(conv_both, lax.dynamic_slice_in_dim(out_full, at, 512, 0), 1, 1)
 
     sends = {step: x_shift(partial(step).astype(BF16), step) for step in (2, 1, 3)}
     total = partial(0)
@@ -153,7 +170,28 @@
     grad_pre = jnp.where(alive, grad_hid, 0.0)
     mid_part = jnp.sum(grad_pre * pre_chip, axis=0).reshape(2, 128)
     grad_act = (grad_pre * mid_gain).astype(BF16)
-    act = gather_x(grad_act, y_hi, core)
+
+    def weight_partial(blocks, beside, a_mine, a_theirs):
+        whole = jnp.zeros((2048, 512), BF16)
+        for step, block in blocks.items():
+            product = dot(block, a_mine, 0, 0) + dot(beside[step], a_theirs, 0, 0)
+            product = product.astype(BF16)
+            for i, y in ((0, y_hi), (1, 1 - y_hi)):
+                whole = lax.dynamic_update_slice_in_dim(
+                    whole,
+                    product[i * 256 : i * 256 + 256],
+                    ((x + step) % 4) * 512 + y * 256,
+                    0,
+                )
+        return whole
+
+    hid_beside = {step: core_swap(block) for step, block in hid.items()}
+    wout = weight_partial(hid, hid_beside, conv_mine, conv_theirs)
+    grad_act, wout = lax.optimization_barrier((grad_act, wout))
+    grad_wout = (
+        lax.psum_scatter(wout, "row", scatter_dimension=0, tiled=True).astype(F32) * scaling
+    )
+    act = gather_x(grad_act, core)
 
     mid_own = lax.dynamic_index_in_dim(mid_part, core, 0, keepdims=False)
     mid_away = lax.dynamic_index_in_dim(mid_part, 1 - core, 0, keepdims=False)
@@ -165,32 +203,22 @@
     grad_smid = keep_mid.astype(F32) * scaling * sums[0]
     grad_swide = keep_wide.astype(F32) * scaling * sums[1:].reshape(512)
 
-    def weight_partial(blocks, a_mine, a_theirs):
-        whole = jnp.zeros((2048, 512), BF16)
-        for step, block in blocks.items():
-            product = dot(block, a_mine, 0, 0) + dot(core_swap(block), a_theirs, 0, 0)
-            whole = lax.dynamic_update_slice_in_dim(
-                whole, product.astype(BF16), ((x + step) % 4) * 512, 0
-            )
-        return whole
-
-    wout = weight_partial(hid, conv_mine, conv_theirs)
-    grad_wout = (
-        lax.psum_scatter(wout, "row", scatter_dimension=0, tiled=True).astype(F32) * scaling
-    )
-
     act_beside = {step: core_swap(block) for step, block in act.items()}
-    win = jnp.zeros((2048, 512), BF16)
-    in_mine, in_theirs = mine(inputs), theirs(inputs)
+    win = weight_partial(act, act_beside, mine(inputs), theirs(inputs))
+    grad_win = (reduce_z(win, z, y_lo) * scaling).T
+    act, act_beside, win = lax.optimization_barrier((act, act_beside, win))
     grad_mine, grad_theirs = mine(cotangent).astype(F32), theirs(cotangent).astype(F32)
     for step, block in act.items():
         at = ((x + step) % 4) * 512
-        product = dot(block, in_mine, 0, 0) + dot(act_beside[step], in_theirs, 0, 0)
-        win = lax.dynamic_update_slice_in_dim(win, product.astype(BF16), at, 0)
-        weights = lax.dynamic_slice_in_dim(in_full, at, 512, 1)
+        weights = jnp.concatenate(
+            [
+                lax.dynamic_slice_in_dim(in_full, at + y * 256, 256, 1)
+                for y in (y_hi, 1 - y_hi)
+            ],
+            axis=1,
+        )
         grad_mine = grad_mine + dot(block, weights, 1, 1)
         grad_theirs = grad_theirs + dot(act_beside[step], weights, 1, 1)
-    grad_win = (reduce_z(win, z, y_lo) * scaling).T
     grad_x = jnp.zeros((rows, width), BF16)
     grad_x = lax.dynamic_update_slice_in_dim(grad_x, grad_mine.astype(BF16), core * half, 0)
     grad_x = lax.dynamic_update_slice_in_dim(

time: 289 us -> 265 us (0.917)
  matrix products: 57.4 us -> 33.7 us
  waiting for transfers between devices: 148 us -> 127 us
  starting transfers between devices: 30.2 us -> 42.8 us
  local copies, waits for them, and re-layouts: 14.6 us -> 25 us
    all_gather x1 -> x0, waiting for transfers between devices: 46.1 us -> none  [local(): out_full = lax.all_gather(weight_out, 'row', axis=0, tiled=True)]
    dot_general x32 -> x28, matrix products: 57.4 us -> 33.7 us  [dot(): lax.dot_general(a, b, (((ca,), (cb,)), ((), ())), preferred_element_type=...]
    ppermute x2, waiting for transfers between devices: 0.01 us -> 10.9 us  [x_split_shift(): lax.ppermute(v, AXES, flat_pairs(lambda yl, z, x, yh, c: (yl, z, x + 1 -...]
    ppermute x2 -> x3, waiting for transfers between devices: 5.2 us -> 13.7 us  [y_lo_swap(): lax.ppermute(v, AXES, flat_pairs(lambda yl, z, x, yh, c: (1 - yl, z, x, y...]
    ppermute x0 -> x1, waiting for transfers between devices: none -> 6.81 us  [z_split_shift(): lax.ppermute(v, AXES, flat_pairs(lambda yl, z, x, yh, c: (yl, z + 1 - 2 *...]
    dynamic_update_slice x0 -> x24, local copies, waits for them, and re-layouts: none -> 6.39 us  [the longest x16 5.97 us: weight_partial(): lax.dynamic_update_slice_in_dim(whole, product[i * 256:i * 256 + 256], (x...]
    ppermute x3 -> x5, waiting for transfers between devices: 32.8 us -> 27 us  [z_shift(): lax.ppermute(v, AXES, flat_pairs(lambda yl, z, x, yh, c: (yl, z + step, x...]
    ppermute x3, waiting for transfers between devices: 8.01 us -> 12.1 us  [y_hi_swap(): lax.ppermute(v, AXES, flat_pairs(lambda yl, z, x, yh, c: (yl, z, x, 1 - y...]
  transfers between devices with their start and end apart: 35 -> 41, of which waited for: 17 -> 21; matrix products, arithmetic and copies ran while one was open for 31% -> 26% of each run, Pallas kernels for 0% -> 0%
where the time goes in v2:
time: 265 us; the launch traced here: 264 us
  waiting for transfers between devices  127 us (48%)
  starting transfers between devices  42.8 us (16%)
  matrix products  33.7 us (13%)
  local copies, waits for them, and re-layouts  25 us (9%)
  other arithmetic  20.7 us (8%)
  between operations  14.8 us (6%)
    ppermute x7, waiting for transfers between devices, x_shift(): lax.ppermute(v, AXES, flat_pairs(lambda yl, z, x, yh, c: (yl, z, x + step...  49.2 us
    dot_general x28, matrix products, dot(): lax.dot_general(a, b, (((ca,), (cb,)), ((), ())), preferred_element_type=...  33.7 us
    ppermute x5, waiting for transfers between devices, z_shift(): lax.ppermute(v, AXES, flat_pairs(lambda yl, z, x, yh, c: (yl, z + step, x...  27 us
    ppermute x3, waiting for transfers between devices, y_lo_swap(): lax.ppermute(v, AXES, flat_pairs(lambda yl, z, x, yh, c: (1 - yl, z, x, y...  13.7 us
    ppermute x7, starting transfers between devices, x_shift(): lax.ppermute(v, AXES, flat_pairs(lambda yl, z, x, yh, c: (yl, z, x + step...  13.5 us
    ppermute x3, waiting for transfers between devices, y_hi_swap(): lax.ppermute(v, AXES, flat_pairs(lambda yl, z, x, yh, c: (yl, z, x, 1 - y...  12.1 us
    ppermute x2, waiting for transfers between devices, x_split_shift(): lax.ppermute(v, AXES, flat_pairs(lambda yl, z, x, yh, c: (yl, z, x + 1 -...  10.9 us
    ppermute x3, starting transfers between devices, y_hi_swap(): lax.ppermute(v, AXES, flat_pairs(lambda yl, z, x, yh, c: (yl, z, x, 1 - y...  9.69 us
  transfers between devices with their start and end apart: 41, of which 21 were waited for; matrix products, arithmetic and copies ran while one was open for 26% of the time, Pallas kernels for 0%

profile of v2, /device:TPU:0, one launch (start us, length us, event | category | flops | bytes accessed | tf_op | source)
XLA Modules:
  0.0 263.7 jit_solution(12772791545390395109)
XLA Ops:
  9.7 5.8 %collective-permute-done.3 = bf16[256,512]{1,0:T(8,128)(2,1)S(1)} collective-permute-done((bf16[256,512]{1,0:T(8,128)(2,1)}, bf16[256,512]{1,0:T(8,128)(2,1)S(1)}, u32[]{:S(2)}, u32[]{:S(2)}) %collective-permute-start.3) | collective-permute-done | bytes 262176 | tf_op jit(solution)/shard_map/ppermute | solution.py:34
  17.4 2.1 collective-permute-start.5
  19.5 2.1 collective-permute-start.7
  21.6 2.6 fusion.1
  25.8 7.1 %collective-permute-done.5 = bf16[2,256,512]{2,1,0:T(8,128)(2,1)} collective-permute-done((bf16[2,256,512]{2,1,0:T(8,128)(2,1)}, bf16[2,256,512]{2,1,0:T(8,128)(2,1)}, u32[]{:S(2)}, u32[]{:S(2)}) %collective-permute-start.5) | collective-permute-done | bytes 524320 | tf_op jit(solution)/shard_map/ppermute | solution.py:48
  38.1 6.8 %collective-permute-done.9 = bf16[2,256,512]{2,1,0:T(8,128)(2,1)S(1)} collective-permute-done((bf16[2,256,512]{2,1,0:T(8,128)(2,1)S(1)}, bf16[2,256,512]{2,1,0:T(8,128)(2,1)S(1)}, u32[]{:S(2)}, u32[]{:S(2)}) %collective-permute-start.9) | collective-permute-done | bytes 524320 | tf_op jit(solution)/shard_map/ppermute | solution.py:68
  47.0 3.7 %convolution_convert_fusion.2 = bf16[768,512]{0,1:T(8,128)(2,1)} fusion(bf16[2048,1024]{1,0:T(8,128)(2,1)S(1)} %bitcast.123, s32[]{:T(128)S(6)} %select_n.310, bf16[768,512]{1,0:T(8,128)(2,1)} %collective-permute-done.2, bf16[768,512]{1,0:T(8,128)(2,1)S(1)} %get-tuple-element.56), kind=kOutput, calls=%fused_computation.10 | convolution fusion | flops 808845312 | bytes 3407876 | tf_op jit(solution)/shard_map/dot_general | solution.py:56
  52.2 3.1 %convolution_convert_fusion.1 = bf16[768,512]{0,1:T(8,128)(2,1)} fusion(bf16[2048,1024]{1,0:T(8,128)(2,1)S(1)} %bitcast.124, s32[]{:T(128)S(6)} %select_n.312, bf16[768,512]{1,0:T(8,128)(2,1)} %collective-permute-done.2, bf16[768,512]{1,0:T(8,128)(2,1)S(1)} %get-tuple-element.56), kind=kOutput, calls=%fused_computation.9 | convolution fusion | flops 808845312 | bytes 3407876 | tf_op jit(solution)/shard_map/dot_general | solution.py:56
  57.0 3.0 %convolution_convert_fusion = bf16[768,512]{0,1:T(8,128)(2,1)} fusion(bf16[2048,1024]{1,0:T(8,128)(2,1)S(1)} %bitcast.125, s32[]{:T(128)S(6)} %select_n.314, bf16[768,512]{1,0:T(8,128)(2,1)} %collective-permute-done.2, bf16[768,512]{1,0:T(8,128)(2,1)S(1)} %get-tuple-element.56), kind=kOutput, calls=%fused_computation.8 | convolution fusion | flops 808845312 | bytes 3407876 | tf_op jit(solution)/shard_map/dot_general | solution.py:56
  64.1 2.5 fusion.15
  66.6 5.1 %collective-permute-done.11 = bf16[768,512]{0,1:T(8,128)(2,1)} collective-permute-done((bf16[768,512]{0,1:T(8,128)(2,1)}, bf16[768,512]{0,1:T(8,128)(2,1)}, u32[]{:S(2)}, u32[]{:S(2)}) %collective-permute-start.11) | collective-permute-done | bytes 786464 | tf_op jit(solution)/shard_map/ppermute | solution.py:38
  71.8 19.2 %collective-permute-done.12 = bf16[768,512]{0,1:T(8,128)(2,1)} collective-permute-done((bf16[768,512]{0,1:T(8,128)(2,1)}, bf16[768,512]{0,1:T(8,128)(2,1)}, u32[]{:S(2)}, u32[]{:S(2)}) %collective-permute-start.12) | collective-permute-done | bytes 786464 | tf_op jit(solution)/shard_map/ppermute | solution.py:38
  91.0 2.0 convert_add_fusion
  95.1 3.2 %collective-permute-start.14 = (bf16[768,256]{1,0:T(8,128)(2,1)}, bf16[768,256]{1,0:T(8,128)(2,1)S(1)}, u32[]{:S(2)}, u32[]{:S(2)}) collective-permute-start(bf16[768,256]{1,0:T(8,128)(2,1)} %bitcast.131), channel_id=1, source_target_pairs={{0,2},{1,3},{2,0},{3,1},{4,6},{5,7},{6,4},{7,5},{8,10},{9,11},{10,... | collective-permute-start | bytes 1179656 | tf_op jit(solution)/shard_map/ppermute | solution.py:30
  100.8 2.1 constant_dynamic-slice_fusion.11
  102.9 2.3 copy.24
  108.2 3.3 %collective-permute-start.15 = (bf16[768,256]{1,0:T(8,128)(2,1)S(1)}, bf16[768,256]{1,0:T(8,128)(2,1)S(1)}, u32[]{:S(2)}, u32[]{:S(2)}) collective-permute-start(bf16[768,256]{1,0:T(8,128)(2,1)S(1)} %get-tuple-element.63), channel_id=1, source_target_pairs={{0,2},{1,3},{2,0},{3,1},{4,6},{5,7},{6,4},{7,5},{8,10},{9,11},{10,... | collective-permute-start | bytes 1179656 | tf_op jit(solution)/shard_map/ppermute | solution.py:30
  111.5 6.4 %collective-permute-done.15 = bf16[768,256]{1,0:T(8,128)(2,1)S(1)} collective-permute-done((bf16[768,256]{1,0:T(8,128)(2,1)S(1)}, bf16[768,256]{1,0:T(8,128)(2,1)S(1)}, u32[]{:S(2)}, u32[]{:S(2)}) %collective-permute-start.15) | collective-permute-done | bytes 393248 | tf_op jit(solution)/shard_map/ppermute | solution.py:30
  118.9 4.8 %collective-permute-start.17 = (bf16[768,512]{1,0:T(8,128)(2,1)}, bf16[768,512]{1,0:T(8,128)(2,1)}, u32[]{:S(2)}, u32[]{:S(2)}) collective-permute-start(bf16[768,512]{1,0:T(8,128)(2,1)} %pad_maximum_fusion.2), channel_id=1, source_target_pairs={{0,4},{1,5},{2,6},{3,7},{4,8},{5,9},{6,10},{7,11},{8,12},{9,13},{1... | collective-permute-start | bytes 2359304 | tf_op jit(solution)/shard_map/ppermute | solution.py:38
  125.3 13.8 %collective-permute-done.17 = bf16[768,512]{1,0:T(8,128)(2,1)} collective-permute-done((bf16[768,512]{1,0:T(8,128)(2,1)}, bf16[768,512]{1,0:T(8,128)(2,1)}, u32[]{:S(2)}, u32[]{:S(2)}) %collective-permute-start.17) | collective-permute-done | bytes 786464 | tf_op jit(solution)/shard_map/ppermute | solution.py:38
  150.1 4.8 %collective-permute-done.21 = bf16[768,512]{1,0:T(8,128)(2,1)S(1)} collective-permute-done((bf16[768,512]{1,0:T(8,128)(2,1)S(1)}, bf16[768,512]{1,0:T(8,128)(2,1)S(1)}, u32[]{:S(2)}, u32[]{:S(2)}) %collective-permute-start.21) | collective-permute-done | bytes 786464 | tf_op jit(solution)/shard_map/ppermute | solution.py:42
  161.8 3.2 %collective-permute-start.23 = (bf16[768,256]{1,0:T(8,128)(2,1)S(1)}, bf16[768,256]{1,0:T(8,128)(2,1)S(1)}, u32[]{:S(2)}, u32[]{:S(2)}) collective-permute-start(bf16[768,256]{1,0:T(8,128)(2,1)S(1)} %get-tuple-element.18), channel_id=1, source_target_pairs={{0,2},{1,3},{2,0},{3,1},{4,6},{5,7},{6,4},{7,5},{8,10},{9,11},{10,... | collective-permute-start | bytes 1179656 | tf_op jit(solution)/shard_map/ppermute | solution.py:30
  165.0 3.6 %collective-permute-done.36 = f32[5,128]{1,0:T(8,128)S(1)} collective-permute-done((f32[5,128]{1,0:T(8,128)S(1)}, f32[5,128]{1,0:T(8,128)S(1)}, u32[]{:S(2)}, u32[]{:S(2)}) %collective-permute-start.36) | collective-permute-done | bytes 2592 | tf_op jit(solution)/shard_map/ppermute | solution.py:52
  171.1 5.1 %collective-permute-done.23 = bf16[768,256]{1,0:T(8,128)(2,1)S(1)} collective-permute-done((bf16[768,256]{1,0:T(8,128)(2,1)S(1)}, bf16[768,256]{1,0:T(8,128)(2,1)S(1)}, u32[]{:S(2)}, u32[]{:S(2)}) %collective-permute-start.23) | collective-permute-done | bytes 393248 | tf_op jit(solution)/shard_map/ppermute | solution.py:30
  178.1 2.1 collective-permute-start.25
  181.9 2.0 collective-permute-done.38
  185.0 2.8 %constant_dynamic-slice_fusion.3 = (bf16[512,256]{1,0:T(8,128)(2,1)S(1)}, bf16[512,256]{1,0:T(8,128)(2,1)}, bf16[512,256]{1,0:T(8,128)(2,1)}, bf16[512,256]{1,0:...) fusion(bf16[512,2048]{1,0:T(8,128)(2,1)} %all-gather.2.cloned.1, ...), kind=kLoop, calls=%fused_computation.139 | loop fusion | bytes 4194336 | tf_op jit(solution)/shard_map/dynamic_slice | solution.py:215
  187.8 9.7 %collective-permute-done.24 = bf16[768,512]{1,0:T(8,128)(2,1)S(1)} collective-permute-done((bf16[768,512]{1,0:T(8,128)(2,1)}, bf16[768,512]{1,0:T(8,128)(2,1)S(1)}, u32[]{:S(2)}, u32[]{:S(2)}) %collective-permute-start.24) | collective-permute-done | bytes 786464 | tf_op jit(solution)/shard_map/ppermute | solution.py:38
  204.8 6.1 %collective-permute-done.26 = bf16[768,512]{1,0:T(8,128)(2,1)S(1)} collective-permute-done((bf16[768,512]{1,0:T(8,128)(2,1)S(1)}, bf16[768,512]{1,0:T(8,128)(2,1)S(1)}, u32[]{:S(2)}, u32[]{:S(2)}) %collective-permute-start.26) | collective-permute-done | bytes 786464 | tf_op jit(solution)/shard_map/ppermute | solution.py:42
  214.2 3.2 %collective-permute-start.32 = (bf16[2,256,512]{2,1,0:T(8,128)(2,1)S(1)}, bf16[2,256,512]{2,1,0:T(8,128)(2,1)S(1)}, u32[]{:S(2)}, u32[]{:S(2)}) collective-permute-start(bf16[2,256,512]{2,1,0:T(8,128)(2,1)S(1)} %get-tuple-element.43), channel_id=1, source_target_pairs={{0,48},{1,49},{2,50},{3,51},{4,52},{5,53},{6,54},{7,55},{8,56},{9,... | collective-permute-start | bytes 1572872 | tf_op jit(solution)/shard_map/ppermute | solution.py:48
  225.4 19.9 %collective-permute-done.31 = bf16[2,256,512]{2,1,0:T(8,128)(2,1)S(1)} collective-permute-done((bf16[2,256,512]{2,1,0:T(8,128)(2,1)S(1)}, bf16[2,256,512]{2,1,0:T(8,128)(2,1)S(1)}, u32[]{:S(2)}, u32[]{:S(2)}) %collective-permute-start.31) | collective-permute-done | bytes 524320 | tf_op jit(solution)/shard_map/ppermute | solution.py:48
  248.1 5.9 %collective-permute-done.34 = bf16[256,512]{1,0:T(8,128)(2,1)S(1)} collective-permute-done((bf16[256,512]{1,0:T(8,128)(2,1)S(1)}, bf16[256,512]{1,0:T(8,128)(2,1)S(1)}, u32[]{:S(2)}, u32[]{:S(2)}) %collective-permute-start.34) | collective-permute-done | bytes 262176 | tf_op jit(solution)/shard_map/ppermute | solution.py:34
  (201 shorter events, 79.5 us)
Async XLA Ops:
  7.2 177.8 %all-gather.2.cloned.1.call-start = ((), (), s32[]{:S(2)}) async-start(), calls=%async_computation.1 | async-start | bytes 2359296 | tf_op jit(solution)/shard_map/all_gather | solution.py:155
  17.4 15.6 %collective-permute-start.5 = (bf16[2,256,512]{2,1,0:T(8,128)(2,1)}, bf16[2,256,512]{2,1,0:T(8,128)(2,1)}, u32[]{:S(2)}, u32[]{:S(2)}) collective-permute-start(bf16[2,256,512]{2,1,0:T(8,128)(2,1)} %pad_maximum_fusion.3), channel_id=1, source_target_pairs={{0,16},{1,17},{2,18},{3,19},{4,20},{5,21},{6,22},{7,23},{8,24},{9,... | collective-permute-start | bytes 1572872 | tf_op jit(solution)/shard_map/ppermute | solution.py:48
  19.5 13.5 %collective-permute-start.7 = (bf16[2,256,512]{2,1,0:T(8,128)(2,1)}, bf16[2,256,512]{2,1,0:T(8,128)(2,1)}, u32[]{:S(2)}, u32[]{:S(2)}) collective-permute-start(bf16[2,256,512]{2,1,0:T(8,128)(2,1)} %pad_maximum_fusion.3), channel_id=1, source_target_pairs={{0,48},{1,49},{2,50},{3,51},{4,52},{5,53},{6,54},{7,55},{8,56},{9,... | collective-permute-start | bytes 1572872 | tf_op jit(solution)/shard_map/ppermute | solution.py:48
  24.1 11.6 %collective-permute-start.4 = (bf16[2,256,512]{2,1,0:T(8,128)(2,1)}, bf16[2,256,512]{2,1,0:T(8,128)(2,1)}, u32[]{:S(2)}, u32[]{:S(2)}) collective-permute-start(bf16[2,256,512]{2,1,0:T(8,128)(2,1)} %pad_maximum_fusion.3), channel_id=1, source_target_pairs={{0,1},{1,0},{2,3},{3,2},{4,5},{5,4},{6,7},{7,6},{8,9},{9,8},{10,11... | collective-permute-start | bytes 1572872 | tf_op jit(solution)/shard_map/ppermute | solution.py:26
  24.4 22.6 %collective-permute-start.2 = (bf16[768,512]{1,0:T(8,128)(2,1)S(1)}, bf16[768,512]{1,0:T(8,128)(2,1)}, u32[]{:S(2)}, u32[]{:S(2)}) collective-permute-start(bf16[768,512]{1,0:T(8,128)(2,1)S(1)} %get-tuple-element.57), channel_id=1, source_target_pairs={{0,1},{1,0},{2,3},{3,2},{4,5},{5,4},{6,7},{7,6},{8,9},{9,8},{10,11... | collective-permute-start | bytes 2359304 | tf_op jit(solution)/shard_map/ppermute | solution.py:26
  25.8 73.1 %collective-permute-start = (bf16[768,128]{1,0:T(8,128)(2,1)}, bf16[768,128]{1,0:T(8,128)(2,1)}, u32[]{:S(2)}, u32[]{:S(2)}) collective-permute-start(bf16[768,128]{1,0:T(8,128)(2,1)} %constant_dynamic-slice_fusion.14), channel_id=1, source_target_pairs={{0,1},{1,0},{2,3},{3,2},{4,5},{5,4},{6,7},{7,6},{8,9},{9,8},{10,11... | collective-permute-start | bytes 589832 | tf_op jit(solution)/shard_map/ppermute | solution.py:26
  34.4 10.5 %collective-permute-start.9 = (bf16[2,256,512]{2,1,0:T(8,128)(2,1)S(1)}, bf16[2,256,512]{2,1,0:T(8,128)(2,1)S(1)}, u32[]{:S(2)}, u32[]{:S(2)}) collective-permute-start(bf16[2,256,512]{2,1,0:T(8,128)(2,1)S(1)} %get-tuple-element.60), channel_id=1, source_target_pairs={{0,16},{1,49},{2,18},{3,51},{4,20},{5,53},{6,22},{7,55},{8,24},{9,... | collective-permute-start | bytes 1572872 | tf_op jit(solution)/shard_map/ppermute | solution.py:68
  35.7 9.1 %collective-permute-start.6 = (bf16[2,256,512]{2,1,0:T(8,128)(2,1)}, bf16[2,256,512]{2,1,0:T(8,128)(2,1)S(1)}, u32[]{:S(2)}, u32[]{:S(2)}) collective-permute-start(bf16[2,256,512]{2,1,0:T(8,128)(2,1)} %collective-permute-done.5), channel_id=1, source_target_pairs={{0,1},{1,0},{2,3},{3,2},{4,5},{5,4},{6,7},{7,6},{8,9},{9,8},{10,11... | collective-permute-start | bytes 1572872 | tf_op jit(solution)/shard_map/ppermute | solution.py:26
  35.7 9.3 %collective-permute-start.8 = (bf16[2,256,512]{2,1,0:T(8,128)(2,1)}, bf16[2,256,512]{2,1,0:T(8,128)(2,1)S(1)}, u32[]{:S(2)}, u32[]{:S(2)}) collective-permute-start(bf16[2,256,512]{2,1,0:T(8,128)(2,1)} %collective-permute-done.7), channel_id=1, source_target_pairs={{0,1},{1,0},{2,3},{3,2},{4,5},{5,4},{6,7},{7,6},{8,9},{9,8},{10,11... | collective-permute-start | bytes 1572872 | tf_op jit(solution)/shard_map/ppermute | solution.py:26
  50.7 21.1 %collective-permute-start.11 = (bf16[768,512]{0,1:T(8,128)(2,1)}, bf16[768,512]{0,1:T(8,128)(2,1)}, u32[]{:S(2)}, u32[]{:S(2)}) collective-permute-start(bf16[768,512]{0,1:T(8,128)(2,1)} %convolution_convert_fusion.2), channel_id=1, source_target_pairs={{0,4},{1,5},{2,6},{3,7},{4,8},{5,9},{6,10},{7,11},{8,12},{9,13},{1... | collective-permute-start | bytes 2359304 | tf_op jit(solution)/shard_map/ppermute | solution.py:38
  55.2 35.8 %collective-permute-start.12 = (bf16[768,512]{0,1:T(8,128)(2,1)}, bf16[768,512]{0,1:T(8,128)(2,1)}, u32[]{:S(2)}, u32[]{:S(2)}) collective-permute-start(bf16[768,512]{0,1:T(8,128)(2,1)} %convolution_convert_fusion.1), channel_id=1, source_target_pairs={{0,12},{1,13},{2,14},{3,15},{4,0},{5,1},{6,2},{7,3},{8,4},{9,5},{1... | collective-permute-start | bytes 2359304 | tf_op jit(solution)/shard_map/ppermute | solution.py:38
  60.0 31.0 %collective-permute-start.13 = (bf16[768,512]{0,1:T(8,128)(2,1)}, bf16[768,512]{0,1:T(8,128)(2,1)}, u32[]{:S(2)}, u32[]{:S(2)}) collective-permute-start(bf16[768,512]{0,1:T(8,128)(2,1)} %convolution_convert_fusion), channel_id=1, source_target_pairs={{0,8},{1,9},{2,10},{3,11},{4,12},{5,13},{6,14},{7,15},{8,0},{9,1},... | collective-permute-start | bytes 2359304 | tf_op jit(solution)/shard_map/ppermute | solution.py:38
  95.1 10.7 %collective-permute-start.14 = (bf16[768,256]{1,0:T(8,128)(2,1)}, bf16[768,256]{1,0:T(8,128)(2,1)S(1)}, u32[]{:S(2)}, u32[]{:S(2)}) collective-permute-start(bf16[768,256]{1,0:T(8,128)(2,1)} %bitcast.131), channel_id=1, source_target_pairs={{0,2},{1,3},{2,0},{3,1},{4,6},{5,7},{6,4},{7,5},{8,10},{9,11},{10,... | collective-permute-start | bytes 1179656 | tf_op jit(solution)/shard_map/ppermute | solution.py:30
  108.2 9.7 %collective-permute-start.15 = (bf16[768,256]{1,0:T(8,128)(2,1)S(1)}, bf16[768,256]{1,0:T(8,128)(2,1)S(1)}, u32[]{:S(2)}, u32[]{:S(2)}) collective-permute-start(bf16[768,256]{1,0:T(8,128)(2,1)S(1)} %get-tuple-element.63), channel_id=1, source_target_pairs={{0,2},{1,3},{2,0},{3,1},{4,6},{5,7},{6,4},{7,5},{8,10},{9,11},{10,... | collective-permute-start | bytes 1179656 | tf_op jit(solution)/shard_map/ppermute | solution.py:30
  118.9 20.1 %collective-permute-start.17 = (bf16[768,512]{1,0:T(8,128)(2,1)}, bf16[768,512]{1,0:T(8,128)(2,1)}, u32[]{:S(2)}, u32[]{:S(2)}) collective-permute-start(bf16[768,512]{1,0:T(8,128)(2,1)} %pad_maximum_fusion.2), channel_id=1, source_target_pairs={{0,4},{1,5},{2,6},{3,7},{4,8},{5,9},{6,10},{7,11},{8,12},{9,13},{1... | collective-permute-start | bytes 2359304 | tf_op jit(solution)/shard_map/ppermute | solution.py:38
  123.8 16.6 %collective-permute-start.19 = (bf16[768,512]{1,0:T(8,128)(2,1)}, bf16[768,512]{1,0:T(8,128)(2,1)}, u32[]{:S(2)}, u32[]{:S(2)}) collective-permute-start(bf16[768,512]{1,0:T(8,128)(2,1)} %pad_maximum_fusion.2), channel_id=1, source_target_pairs={{0,12},{1,13},{2,14},{3,15},{4,0},{5,1},{6,2},{7,3},{8,4},{9,5},{1... | collective-permute-start | bytes 2359304 | tf_op jit(solution)/shard_map/ppermute | solution.py:38
  124.2 130.8 %reduce-scatter.2.cloned.1.call-start = ((), (), s32[]{:S(2)}) async-start(), calls=%async_computation.2 | async-start | bytes 2359296 | tf_op jit(solution)/shard_map/reduce_scatter | solution.py:192
  124.3 20.0 %collective-permute-start.16 = (bf16[768,512]{1,0:T(8,128)(2,1)}, bf16[768,512]{1,0:T(8,128)(2,1)S(1)}, u32[]{:S(2)}, u32[]{:S(2)}) collective-permute-start(bf16[768,512]{1,0:T(8,128)(2,1)} %pad_maximum_fusion.2), channel_id=1, source_target_pairs={{0,1},{1,0},{2,3},{3,2},{4,5},{5,4},{6,7},{7,6},{8,9},{9,8},{10,11... | collective-permute-start | bytes 2359304 | tf_op jit(solution)/shard_map/ppermute | solution.py:26
  141.7 13.3 %collective-permute-start.21 = (bf16[768,512]{1,0:T(8,128)(2,1)S(1)}, bf16[768,512]{1,0:T(8,128)(2,1)S(1)}, u32[]{:S(2)}, u32[]{:S(2)}) collective-permute-start(bf16[768,512]{1,0:T(8,128)(2,1)S(1)} %broadcast_select_fusion.1), channel_id=1, source_target_pairs={{0,4},{1,13},{2,6},{3,15},{4,8},{5,1},{6,10},{7,3},{8,12},{9,5},{1... | collective-permute-start | bytes 2359304 | tf_op jit(solution)/shard_map/ppermute | solution.py:42
  142.0 14.3 %collective-permute-start.20 = (bf16[768,512]{1,0:T(8,128)(2,1)}, bf16[768,512]{1,0:T(8,128)(2,1)S(1)}, u32[]{:S(2)}, u32[]{:S(2)}) collective-permute-start(bf16[768,512]{1,0:T(8,128)(2,1)} %collective-permute-done.19), channel_id=1, source_target_pairs={{0,1},{1,0},{2,3},{3,2},{4,5},{5,4},{6,7},{7,6},{8,9},{9,8},{10,11... | collective-permute-start | bytes 2359304 | tf_op jit(solution)/shard_map/ppermute | solution.py:26
  142.0 12.9 %collective-permute-start.18 = (bf16[768,512]{1,0:T(8,128)(2,1)}, bf16[768,512]{1,0:T(8,128)(2,1)S(1)}, u32[]{:S(2)}, u32[]{:S(2)}) collective-permute-start(bf16[768,512]{1,0:T(8,128)(2,1)} %collective-permute-done.17), channel_id=1, source_target_pairs={{0,1},{1,0},{2,3},{3,2},{4,5},{5,4},{6,7},{7,6},{8,9},{9,8},{10,11... | collective-permute-start | bytes 2359304 | tf_op jit(solution)/shard_map/ppermute | solution.py:26
  161.8 14.4 %collective-permute-start.23 = (bf16[768,256]{1,0:T(8,128)(2,1)S(1)}, bf16[768,256]{1,0:T(8,128)(2,1)S(1)}, u32[]{:S(2)}, u32[]{:S(2)}) collective-permute-start(bf16[768,256]{1,0:T(8,128)(2,1)S(1)} %get-tuple-element.18), channel_id=1, source_target_pairs={{0,2},{1,3},{2,0},{3,1},{4,6},{5,7},{6,4},{7,5},{8,10},{9,11},{10,... | collective-permute-start | bytes 1179656 | tf_op jit(solution)/shard_map/ppermute | solution.py:30
  168.6 11.6 %collective-permute-start.37 = (f32[5,128]{1,0:T(8,128)S(1)}, f32[5,128]{1,0:T(8,128)S(1)}, u32[]{:S(2)}, u32[]{:S(2)}) collective-permute-start(f32[5,128]{1,0:T(8,128)S(1)} %fusion.72), channel_id=1, source_target_pairs={{0,32},{1,33},{2,34},{3,35},{4,36},{5,37},{6,38},{7,39},{8,40},{9,... | collective-permute-start | bytes 7688 | tf_op jit(solution)/shard_map/ppermute | solution.py:52
  177.0 20.6 %collective-permute-start.24 = (bf16[768,512]{1,0:T(8,128)(2,1)}, bf16[768,512]{1,0:T(8,128)(2,1)S(1)}, u32[]{:S(2)}, u32[]{:S(2)}) collective-permute-start(bf16[768,512]{1,0:T(8,128)(2,1)} %constant_dynamic-update-slice_fusion.6), channel_id=1, source_target_pairs={{0,4},{1,5},{2,6},{3,7},{4,8},{5,9},{6,10},{7,11},{8,12},{9,13},{1... | collective-permute-start | bytes 2359304 | tf_op jit(solution)/shard_map/ppermute | solution.py:38
  178.1 19.5 %collective-permute-start.25 = (bf16[768,512]{1,0:T(8,128)(2,1)}, bf16[768,512]{1,0:T(8,128)(2,1)S(1)}, u32[]{:S(2)}, u32[]{:S(2)}) collective-permute-start(bf16[768,512]{1,0:T(8,128)(2,1)} %constant_dynamic-update-slice_fusion.6), channel_id=1, source_target_pairs={{0,12},{1,13},{2,14},{3,15},{4,0},{5,1},{6,2},{7,3},{8,4},{9,5},{1... | collective-permute-start | bytes 2359304 | tf_op jit(solution)/shard_map/ppermute | solution.py:38
  183.9 15.1 %collective-permute-start.28 = (bf16[768,512]{1,0:T(8,128)(2,1)}, bf16[768,512]{1,0:T(8,128)(2,1)}, u32[]{:S(2)}, u32[]{:S(2)}) collective-permute-start(bf16[768,512]{1,0:T(8,128)(2,1)} %constant_dynamic-update-slice_fusion.6), channel_id=1, source_target_pairs={{0,1},{1,0},{2,3},{3,2},{4,5},{5,4},{6,7},{7,6},{8,9},{9,8},{10,11... | collective-permute-start | bytes 2359304 | tf_op jit(solution)/shard_map/ppermute | solution.py:26
  197.7 13.3 %collective-permute-start.26 = (bf16[768,512]{1,0:T(8,128)(2,1)S(1)}, bf16[768,512]{1,0:T(8,128)(2,1)S(1)}, u32[]{:S(2)}, u32[]{:S(2)}) collective-permute-start(bf16[768,512]{1,0:T(8,128)(2,1)S(1)} %broadcast_select_fusion), channel_id=1, source_target_pairs={{0,4},{1,13},{2,6},{3,15},{4,8},{5,1},{6,10},{7,3},{8,12},{9,5},{1... | collective-permute-start | bytes 2359304 | tf_op jit(solution)/shard_map/ppermute | solution.py:42
  202.5 8.4 %collective-permute-start.27 = (bf16[768,512]{1,0:T(8,128)(2,1)S(1)}, bf16[768,512]{1,0:T(8,128)(2,1)S(1)}, u32[]{:S(2)}, u32[]{:S(2)}) collective-permute-start(bf16[768,512]{1,0:T(8,128)(2,1)S(1)} %collective-permute-done.24), channel_id=1, source_target_pairs={{0,1},{1,0},{2,3},{3,2},{4,5},{5,4},{6,7},{7,6},{8,9},{9,8},{10,11... | collective-permute-start | bytes 2359304 | tf_op jit(solution)/shard_map/ppermute | solution.py:26
  202.8 8.8 %collective-permute-start.29 = (bf16[768,512]{1,0:T(8,128)(2,1)S(1)}, bf16[768,512]{1,0:T(8,128)(2,1)S(1)}, u32[]{:S(2)}, u32[]{:S(2)}) collective-permute-start(bf16[768,512]{1,0:T(8,128)(2,1)S(1)} %collective-permute-done.25), channel_id=1, source_target_pairs={{0,1},{1,0},{2,3},{3,2},{4,5},{5,4},{6,7},{7,6},{8,9},{9,8},{10,11... | collective-permute-start | bytes 2359304 | tf_op jit(solution)/shard_map/ppermute | solution.py:26
  214.1 31.2 %collective-permute-start.31 = (bf16[2,256,512]{2,1,0:T(8,128)(2,1)S(1)}, bf16[2,256,512]{2,1,0:T(8,128)(2,1)S(1)}, u32[]{:S(2)}, u32[]{:S(2)}) collective-permute-start(bf16[2,256,512]{2,1,0:T(8,128)(2,1)S(1)} %get-tuple-element.41), channel_id=1, source_target_pairs={{0,16},{1,17},{2,18},{3,19},{4,20},{5,21},{6,22},{7,23},{8,24},{9,... | collective-permute-start | bytes 1572872 | tf_op jit(solution)/shard_map/ppermute | solution.py:48
  214.2 31.1 %collective-permute-start.32 = (bf16[2,256,512]{2,1,0:T(8,128)(2,1)S(1)}, bf16[2,256,512]{2,1,0:T(8,128)(2,1)S(1)}, u32[]{:S(2)}, u32[]{:S(2)}) collective-permute-start(bf16[2,256,512]{2,1,0:T(8,128)(2,1)S(1)} %get-tuple-element.43), channel_id=1, source_target_pairs={{0,48},{1,49},{2,50},{3,51},{4,52},{5,53},{6,54},{7,55},{8,56},{9,... | collective-permute-start | bytes 1572872 | tf_op jit(solution)/shard_map/ppermute | solution.py:48
  217.4 27.9 %collective-permute-start.33 = (bf16[2,256,512]{2,1,0:T(8,128)(2,1)S(1)}, bf16[2,256,512]{2,1,0:T(8,128)(2,1)S(1)}, u32[]{:S(2)}, u32[]{:S(2)}) collective-permute-start(bf16[2,256,512]{2,1,0:T(8,128)(2,1)S(1)} %get-tuple-element.42), channel_id=1, source_target_pairs={{0,32},{1,33},{2,34},{3,35},{4,36},{5,37},{6,38},{7,39},{8,40},{9,... | collective-permute-start | bytes 1572872 | tf_op jit(solution)/shard_map/ppermute | solution.py:48
  (34 other events, 365.9 us)
Sparse Core Ops, SparseCore 0:
  124.3 46.7 all-gather.1
  188.0 40.7 reduce-scatter.1

commit v3 on v1

v3 whole, which is shorter than its diff:
```python
import math

import jax
import jax.numpy as jnp
from jax import lax
from jax.experimental import pallas as pl
from jax.experimental.pallas import tpu as pltpu
from jax.sharding import PartitionSpec as P

F32 = jnp.float32
BF16 = jnp.bfloat16
AXES = ("row", "col")
STEPS = (0, 1, 3, 2)


def permute(v, target):
    pairs = []
    for row in range(8):
        for col in range(16):
            y_lo, z, x, y_hi, core = target(
                row // 4, row % 4, col // 4, (col // 2) % 2, col % 2
            )
            pairs.append(
                (row * 16 + col, (y_lo * 4 + z % 4) * 16 + (x % 4) * 4 + y_hi * 2 + core)
            )
    return lax.ppermute(v, AXES, pairs)


def core_swap(v):
    return permute(v, lambda yl, z, x, yh, c: (yl, z, x, yh, 1 - c))


def y_hi_swap(v):
    return permute(v, lambda yl, z, x, yh, c: (yl, z, x, 1 - yh, c))


def y_lo_swap(v):
    return permute(v, lambda yl, z, x, yh, c: (1 - yl, z, x, yh, c))


def z_flip(v, mask):
    return permute(v, lambda yl, z, x, yh, c: (yl, z ^ mask, x, yh, c))


def x_shift(v, step):
    return permute(v, lambda yl, z, x, yh, c: (yl, z, x + step, yh, c))


def z_shift(v, step):
    return permute(v, lambda yl, z, x, yh, c: (yl, z + step, x, yh, c))


def x_split(v, way):
    return permute(v, lambda yl, z, x, yh, c: (yl, z, x + way * (1 - 2 * c), yh, c))


def z_split(v, way):
    return permute(v, lambda yl, z, x, yh, c: (yl, z + way * (1 - 2 * c), x, yh, c))


def dot(a, b, ca, cb):
    return lax.dot_general(a, b, (((ca,), (cb,)), ((), ())), preferred_element_type=F32)


def gather(block, core, swap, shift, split):
    here = jnp.stack([block, swap(block)])
    below = shift(here, 1)
    above = shift(here, -1)
    return [here, above, below, split(jnp.where(core == 0, below, above), 1)]


def load_blocks(refs, held, sems):
    half = held.shape[2] // 2
    copies = []
    for k, ref in enumerate(refs):
        copies.append(
            pltpu.make_async_copy(
                ref, held.at[k % 4, :, pl.ds((k // 4) * half, half), :], sems.at[k]
            )
        )
    for copy in copies:
        copy.start()
    for copy in copies:
        copy.wait()


def weight_kernel(place, left, *refs):
    blocks, outs, (held, sems) = refs[:8], refs[8:12], refs[12:]
    load_blocks(blocks, held, sems)
    for o, out in enumerate(outs):
        for i in range(2):
            at = o * 2 + i
            block = held[place[at, 0], place[at, 1]]
            out[i] = jnp.dot(left[...], block, preferred_element_type=F32).astype(BF16)


def weight_partial(place, left, mine, beside):
    any_space = pl.BlockSpec(memory_space=pl.ANY)
    vmem = pl.BlockSpec(memory_space=pltpu.VMEM)
    return pl.pallas_call(
        weight_kernel,
        out_shape=[jax.ShapeDtypeStruct((2, 512, 256), BF16)] * 4,
        in_specs=[pl.BlockSpec(memory_space=pltpu.SMEM), vmem] + [any_space] * 8,
        out_specs=[vmem] * 4,
        scratch_shapes=[pltpu.VMEM((4, 2, 1536, 256), BF16), pltpu.SemaphoreType.DMA((8,))],
        compiler_params=pltpu.CompilerParams(vmem_limit_bytes=32 * 1024 * 1024),
        cost_estimate=pl.CostEstimate(
            flops=2 * 1536 * 512 * 2048, bytes_accessed=10 * 1024 * 1024, transcendentals=0
        ),
    )(place, left, *mine, *beside)


def out_kernel(place, weights, cot, *refs):
    blocks, out, (held, sems) = refs[:8], refs[8], refs[9:]
    load_blocks(blocks, held, sems)
    tile = 256
    for part in range(2):
        start = place[8 + part, 0] * 768
        for t in range(3):
            at = pl.multiple_of(start + t * tile, tile)
            total = cot[pl.ds(at, tile), :].astype(F32)
            for k in range(8):
                columns = pl.ds(pl.multiple_of(place[k, 0] * 256, 256), 256)
                total = total + lax.dot_general(
                    held[k // 2, k % 2, pl.ds(part * 768 + t * tile, tile), :],
                    weights[:, columns],
                    (((1,), (1,)), ((), ())),
                    preferred_element_type=F32,
                )
            out[pl.ds(at, tile), :] = total.astype(BF16)


def out_gradient(place, weights, cot, mine, beside):
    any_space = pl.BlockSpec(memory_space=pl.ANY)
    vmem = pl.BlockSpec(memory_space=pltpu.VMEM)
    return pl.pallas_call(
        out_kernel,
        out_shape=jax.ShapeDtypeStruct((1536, 512), BF16),
        in_specs=[pl.BlockSpec(memory_space=pltpu.SMEM), vmem, vmem] + [any_space] * 8,
        out_specs=vmem,
        scratch_shapes=[pltpu.VMEM((4, 2, 1536, 256), BF16), pltpu.SemaphoreType.DMA((8,))],
        compiler_params=pltpu.CompilerParams(vmem_limit_bytes=32 * 1024 * 1024),
        cost_estimate=pl.CostEstimate(
            flops=2 * 1536 * 512 * 2048, bytes_accessed=12 * 1024 * 1024, transcendentals=0
        ),
    )(place, weights, cot, *mine, *beside)


def reduce(away, there, onward, here, split):
    passed = split(away, 1)
    back = split(there, -1)
    onward = (onward + passed.astype(F32)).astype(BF16)
    return here + back.astype(F32) + split(onward, 1).astype(F32)


def local(
    inputs,
    cotangent,
    conv_out,
    pre_act,
    weight_in,
    weight_out,
    scale_mid,
    scale_wide,
    keep_mid,
    keep_wide,
):
    rows = inputs.shape[0]
    half = rows // 2
    scaling = 1.0 / math.sqrt(rows * lax.axis_size("row"))
    row, col = lax.axis_index("row"), lax.axis_index("col")
    y_lo, z = row // 4, row % 4
    x, y_hi, core = col // 4, (col // 2) % 2, col % 2
    ahead = 1 - 2 * core

    def mine(v):
        return lax.dynamic_slice_in_dim(v, core * half, half, 0)

    def theirs(v):
        return lax.dynamic_slice_in_dim(v, (1 - core) * half, half, 0)

    def halves(v):
        return jnp.concatenate([mine(v), theirs(v)], axis=0)

    out_blocks = gather(weight_out, core, y_lo_swap, z_shift, z_split)

    gain_pair = jnp.stack([scale_mid, keep_mid.astype(F32)])
    gain_beside = core_swap(gain_pair)
    pre_mine = mine(pre_act)
    pre_beside = core_swap(theirs(pre_act))

    def chip_order(a, b):
        return jnp.concatenate(
            [jnp.where(core == 0, a, b), jnp.where(core == 0, b, a)], axis=1
        )

    pre_chip = chip_order(pre_mine, pre_beside).astype(F32)
    gain_chip = chip_order(gain_pair, gain_beside)
    mid_gain = gain_chip[0] * gain_chip[1]
    hidden = jnp.maximum(pre_chip * mid_gain, 0.0).astype(BF16)
    hid = gather(hidden, core, y_hi_swap, x_shift, x_split)

    wide_gain = scale_wide * keep_wide.astype(F32)
    cot_float = cotangent.astype(F32)
    grad_conv = (cot_float * wide_gain).astype(BF16)
    wide_part = jnp.sum(cot_float * conv_out.astype(F32), axis=0)
    conv_mine, conv_theirs = mine(grad_conv), theirs(grad_conv)
    conv_both = jnp.concatenate([conv_mine, core_swap(conv_theirs)], axis=1)

    out_full = jnp.zeros((2, 4, 256, 1024), BF16)
    for step, block in zip(STEPS, out_blocks):
        wide = jnp.concatenate([block, core_swap(block)], axis=2)
        for i, at in ((0, y_lo), (1, 1 - y_lo)):
            out_full = lax.dynamic_update_slice(
                out_full, wide[i][None, None], (at, (z + step) % 4, 0, 0)
            )
    out_full = out_full.reshape(2048, 1024)
    out_full, weight_in, hid[0], hid[1], hid[2] = lax.optimization_barrier(
        (out_full, weight_in, hid[0], hid[1], hid[2])
    )
    in_full = lax.all_gather(weight_in, "row", axis=1, tiled=True)

    def partial(step):
        at = ((x + step) % 4) * 512
        return dot(conv_both, lax.dynamic_slice_in_dim(out_full, at, 512, 0), 1, 1)

    hid_beside = [core_swap(block) for block in hid]

    def block_of(row_z, row_y):
        step = (row_y * 2 + row_z // 2 - x) % 4
        slot = jnp.array([0, 1, 3, 2], jnp.int32)[step]
        return jnp.stack([slot, (row_z % 2) ^ y_hi])

    send_place = jnp.stack(
        [
            block_of((z + step) % 4, y_lo ^ i)
            for step in (2, -ahead, ahead, 0)
            for i in range(2)
        ]
    ).astype(jnp.int32)
    natural = [((x + step) % 4) * 2 + (y_hi ^ i) for step in STEPS for i in range(2)]
    out_place = jnp.stack([jnp.stack(natural + [core, 1 - core]), jnp.zeros(10, jnp.int32)], 1)
    out_place = out_place.astype(jnp.int32)
    scatter_place = jnp.stack(
        [block_of(r % 4, jnp.int32(r // 4)) for r in range(8)]
    ).astype(jnp.int32)

    wout = weight_partial(
        scatter_place,
        jnp.concatenate([conv_mine, conv_theirs], axis=0).T,
        hid,
        hid_beside,
    )
    total = reduce(
        partial(2).astype(BF16), partial(-ahead).astype(BF16), partial(ahead), partial(0), x_split
    )
    total = total.reshape(half, 2, 256)
    own = lax.dynamic_index_in_dim(total, y_hi, 1, keepdims=False)
    away = lax.dynamic_index_in_dim(total, 1 - y_hi, 1, keepdims=False)
    grad_hid = own + y_hi_swap(away.astype(BF16)).astype(F32)
    alive = (pre_chip > 0) & (gain_chip[1] > 0)[None, :]
    grad_pre = jnp.where(alive, grad_hid, 0.0)
    mid_part = jnp.sum(grad_pre * pre_chip, axis=0).reshape(2, 128)
    grad_act = (grad_pre * mid_gain).astype(BF16)
    grad_act, wout, in_full = lax.optimization_barrier((grad_act, wout, in_full))
    wout = lax.psum_scatter(
        jnp.concatenate(wout, axis=0), "row", scatter_dimension=0, tiled=False
    )
    act = gather(grad_act, core, y_hi_swap, x_shift, x_split)

    mid_own = lax.dynamic_index_in_dim(mid_part, core, 0, keepdims=False)
    mid_away = lax.dynamic_index_in_dim(mid_part, 1 - core, 0, keepdims=False)
    mid_own = mid_own + core_swap(mid_away)
    sums = jnp.concatenate([mid_own, wide_part]).reshape(5, 128)
    sums = sums + z_flip(sums, 1)
    sums = sums + z_flip(sums, 2)
    sums = sums + y_lo_swap(sums)
    grad_smid = keep_mid.astype(F32) * scaling * sums[0]
    grad_swide = keep_wide.astype(F32) * scaling * sums[1:].reshape(512)

    act_beside = [core_swap(block) for block in act]
    win = weight_partial(send_place, halves(inputs).T, act, act_beside)
    total = reduce(win[0], win[1], win[2].astype(F32), win[3].astype(F32), z_split)
    act, act_beside, win, wout = lax.optimization_barrier((act, act_beside, win, wout))
    grad_win = (total[0] + y_lo_swap(total[1].astype(BF16)).astype(F32)) * scaling
    grad_wout = wout.astype(F32).T * scaling
    grad_x = out_gradient(out_place, in_full, cotangent, act, act_beside)
    return (grad_x, grad_win, grad_wout, grad_smid, grad_swide)


def solution(mesh):
    return jax.shard_map(
        local,
        mesh=mesh,
        in_specs=(
            P("row", "col"),
            P("row", "col"),
            P("row", "col"),
            P("row", "col"),
            P("col", "row"),
            P("row", "col"),
            P("col"),
            P("col"),
            P("col"),
            P("col"),
        ),
        out_specs=(P("row", "col"), P("col", "row"), P("row", "col"), P("col"), P("col")),
        check_vma=False,
    )
```

time: 289 us -> 252 us (0.87)
  waiting for transfers between devices: 148 us -> 98.4 us
  matrix products: 57.4 us -> 12.7 us
  local copies, waits for them, and re-layouts: 14.6 us -> 35.8 us
  Pallas kernels: 0 us -> 20.4 us
  other arithmetic: 22.9 us -> 36.1 us
    all_gather x1 -> x0, waiting for transfers between devices: 46.1 us -> none  [local(): out_full = lax.all_gather(weight_out, 'row', axis=0, tiled=True)]
    dot_general x32 -> x4, matrix products: 57.4 us -> 12.7 us  [dot(): lax.dot_general(a, b, (((ca,), (cb,)), ((), ())), preferred_element_type=...]
    pallas_call x0 -> x3, Pallas kernels: none -> 20.4 us  [the longest x2 12.8 us: weight_partial(): pl.pallas_call(weight_kernel, out_shape=[jax.ShapeDtypeStruct((2, 512, 25...]
    unnamed x52 -> x61, local copies, waits for them, and re-layouts: 6.61 us -> 20.9 us
    another operation x0 -> x11, other arithmetic: none -> 11.9 us  [the longest x4 5.21 us: local(): jnp.stack([block_of((z + step) % 4, y_lo ^ i) for step in (2, -ahead, ahe...]
    dynamic_update_slice x0 -> x8, local copies, waits for them, and re-layouts: none -> 6.75 us  [local(): lax.dynamic_update_slice(out_full, wide[i][None, None], (at, (z + step) %...]
    dynamic_slice x2, local copies, waits for them, and re-layouts: 4.36 us -> 0.32 us  [local(): own = lax.dynamic_index_in_dim(total, y_hi, 1, keepdims=False)]
    dynamic_slice x0 -> x3, local copies, waits for them, and re-layouts: none -> 3.16 us  [the longest x2 2.47 us: mine(): return lax.dynamic_slice_in_dim(v, core * half, half, 0)]
  transfers between devices with their start and end apart: 35 -> 41, of which waited for: 17 -> 17; matrix products, arithmetic and copies ran while one was open for 31% -> 28% of each run, Pallas kernels for 0% -> 5%
where the time goes in v3:
time: 252 us; the launch traced here: 251 us
  waiting for transfers between devices  98.4 us (39%)
  other arithmetic  36.1 us (14%)
  local copies, waits for them, and re-layouts  35.8 us (14%)
  starting transfers between devices  32.5 us (13%)
  Pallas kernels  20.4 us (8%)
  between operations  14.8 us (6%)
  matrix products  12.7 us (5%)
    ppermute x39, waiting for transfers between devices, permute(): return lax.ppermute(v, AXES, pairs)  98.3 us
    ppermute x39, starting transfers between devices, permute(): return lax.ppermute(v, AXES, pairs)  32.4 us
    unnamed x61, local copies, waits for them, and re-layouts  20.9 us
    pallas_call x2, Pallas kernels, weight_partial(): pl.pallas_call(weight_kernel, out_shape=[jax.ShapeDtypeStruct((2, 512, 25...  12.8 us
    dot_general x4, matrix products, dot(): lax.dot_general(a, b, (((ca,), (cb,)), ((), ())), preferred_element_type=...  12.7 us
    pallas_call x1, Pallas kernels, out_gradient(): pl.pallas_call(out_kernel, out_shape=jax.ShapeDtypeStruct((1536, 512), BF...  7.6 us
    dynamic_update_slice x8, local copies, waits for them, and re-layouts, local(): lax.dynamic_update_slice(out_full, wide[i][None, None], (at, (z + step) %...  6.75 us
    another operation x4, other arithmetic, local(): jnp.stack([block_of((z + step) % 4, y_lo ^ i) for step in (2, -ahead, ahe...  5.21 us
  transfers between devices with their start and end apart: 41, of which 17 were waited for; matrix products, arithmetic and copies ran while one was open for 28% of the time, Pallas kernels for 5%

profile of v3, /device:TPU:0, one launch (start us, length us, event | category | flops | bytes accessed | tf_op | source)
XLA Modules:
  0.0 250.8 jit_solution(12817205043650996406)
XLA Ops:
  18.5 2.9 %collective-permute-start.11 = (bf16[768,256]{1,0:T(8,128)(2,1)}, bf16[768,256]{1,0:T(8,128)(2,1)}, u32[]{:S(2)}, u32[]{:S(2)}) collective-permute-start(bf16[768,256]{1,0:T(8,128)(2,1)} %fusion.8), channel_id=1, source_target_pairs={{0,2},{1,3},{2,0},{3,1},{4,6},{5,7},{6,4},{7,5},{8,10},{9,11},{10,... | collective-permute-start | bytes 1179656 | tf_op jit(solution)/shard_map/ppermute | solution.py:26
  25.2 2.1 collective-permute-start.5
  28.8 2.6 %collective-permute-done.11 = bf16[768,256]{1,0:T(8,128)(2,1)} collective-permute-done((bf16[768,256]{1,0:T(8,128)(2,1)}, bf16[768,256]{1,0:T(8,128)(2,1)}, u32[]{:S(2)}, u32[]{:S(2)}) %collective-permute-start.11) | collective-permute-done | bytes 393248 | tf_op jit(solution)/shard_map/ppermute | solution.py:26
  33.4 2.8 %collective-permute-start.12 = (bf16[2,768,256]{2,1,0:T(8,128)(2,1)}, bf16[2,768,256]{2,1,0:T(8,128)(2,1)S(1)}, u32[]{:S(2)}, u32[]{:S(2)}) collective-permute-start(bf16[2,768,256]{2,1,0:T(8,128)(2,1)} %pad_maximum_fusion.3.refs_0_), channel_id=1, source_target_pairs={{0,12},{1,13},{2,14},{3,15},{4,0},{5,1},{6,2},{7,3},{8,4},{9,5},{1... | collective-permute-start | bytes 2359304 | tf_op jit(solution)/shard_map/ppermute | solution.py:26
  36.1 3.3 %collective-permute-done.7 = bf16[2,256,512]{2,1,0:T(8,128)(2,1)} collective-permute-done((bf16[2,256,512]{2,1,0:T(8,128)(2,1)}, bf16[2,256,512]{2,1,0:T(8,128)(2,1)}, u32[]{:S(2)}, u32[]{:S(2)}) %collective-permute-start.7) | collective-permute-done | bytes 524320 | tf_op jit(solution)/shard_map/ppermute | solution.py:26
  43.7 2.5 %broadcast_in_dim.3 = bf16[2,4,256,1024]{3,2,1,0:T(8,128)(2,1)} broadcast(bf16[]{:T(256)} %constant.292.clone.1), dimensions={} | broadcast | bytes 4194306 | tf_op jit(solution)/shard_map/broadcast_in_dim | solution.py:210
  48.4 4.5 %collective-permute-done.9 = bf16[2,256,512]{2,1,0:T(8,128)(2,1)S(1)} collective-permute-done((bf16[2,256,512]{2,1,0:T(8,128)(2,1)S(1)}, bf16[2,256,512]{2,1,0:T(8,128)(2,1)S(1)}, u32[]{:S(2)}, u32[]{:S(2)}) %collective-permute-start.9) | collective-permute-done | bytes 524320 | tf_op jit(solution)/shard_map/ppermute | solution.py:26
  59.6 3.3 %convolution_convert_fusion = bf16[768,512]{0,1:T(8,128)(2,1)} fusion(bf16[2048,1024]{1,0:T(8,128)(2,1)} %bitcast.23, s32[]{:T(128)S(6)} %select_n.388, bf16[768,512]{0,1:T(8,128)(2,1)} %collective-permute-done.2, bf16[768,512]{0,1:T(8,128)(2,1)S(1)} %get-tuple-element.89), kind=kOutput, calls=%fused_computation.10 | convolution fusion | flops 808845312 | bytes 3407876 | tf_op jit(solution)/shard_map/dot_general | solution.py:62
  65.7 3.3 %convolution_convert_fusion.1 = bf16[768,512]{0,1:T(8,128)(2,1)} fusion(bf16[2048,1024]{1,0:T(8,128)(2,1)} %bitcast.23, s32[]{:T(128)S(6)} %select_n.385, bf16[768,512]{0,1:T(8,128)(2,1)} %collective-permute-done.2, bf16[768,512]{0,1:T(8,128)(2,1)S(1)} %get-tuple-element.89), kind=kOutput, calls=%fused_computation.11 | convolution fusion | flops 808845312 | bytes 3407876 | tf_op jit(solution)/shard_map/dot_general | solution.py:62
  71.5 8.1 %collective-permute-done.15 = bf16[768,512]{0,1:T(8,128)(2,1)} collective-permute-done((bf16[768,512]{0,1:T(8,128)(2,1)}, bf16[768,512]{0,1:T(8,128)(2,1)}, u32[]{:S(2)}, u32[]{:S(2)}) %collective-permute-start.15) | collective-permute-done | bytes 786464 | tf_op jit(solution)/shard_map/ppermute | solution.py:26
  79.6 3.5 %add_convert_fusion = bf16[768,512]{0,1:T(8,128)(2,1)} fusion(bf16[768,512]{0,1:T(8,128)(2,1)} %collective-permute-done.15, bf16[2048,1024]{1,0:T(8,128)(2,1)} %bitcast.23, s32[]{:T(128)S(6)} %select_n.387, bf16[768,512]{0,1:T(8,128)(2,1)} %collective-permute-done.2, bf16[768,512]{0,1:T(8,128)(2,1)S(1)} %get-tuple-element.89), kind=kOutput, calls=%fused_computation.9 | convolution fusion | flops 809631744 | bytes 4194308 | tf_op jit(solution)/shard_map/dot_general | solution.py:62
  86.5 6.8 %collective-permute-done.18.refs_3_ = bf16[2,768,256]{2,1,0:T(8,128)(2,1)} collective-permute-done((bf16[2,768,256]{2,1,0:T(8,128)(2,1)}, bf16[2,768,256]{2,1,0:T(8,128)(2,1)}, u32[]{:S(2)}, u32[]{:S(2)}) %collective-permute-start.18) | collective-permute-done | bytes 786464 | tf_op jit(solution)/shard_map/ppermute | solution.py:26
  96.2 2.6 %fusion.5 = f32[768,512]{0,1:T(8,128)S(1)} fusion(bf16[2048,1024]{1,0:T(8,128)(2,1)} %bitcast.23, s32[]{:T(128)S(6)} %select_n.383, bf16[768,512]{0,1:T(8,128)(2,1)} %collective-permute-done.2, bf16[768,512]{0,1:T(8,128)(2,1)S(1)} %copy-done.17), kind=kOutput, calls=%fused_computation.21 | convolution fusion | flops 808452096 | bytes 4194308 | tf_op jit(solution)/shard_map/dot_general | solution.py:62
  98.8 3.0 %collective-permute-done.16 = bf16[768,512]{0,1:T(8,128)(2,1)} collective-permute-done((bf16[768,512]{0,1:T(8,128)(2,1)}, bf16[768,512]{0,1:T(8,128)(2,1)}, u32[]{:S(2)}, u32[]{:S(2)}) %collective-permute-start.16) | collective-permute-done | bytes 786464 | tf_op jit(solution)/shard_map/ppermute | solution.py:26
  107.7 6.4 %shard_map.281 = (bf16[2,512,256]{2,1,0:T(8,128)(2,1)S(1)}, bf16[2,512,256]{2,1,0:T(8,128)(2,1)S(1)}, bf16[2,512,256]{2,1,0:T(8,128)(2,1)S(1)}, bf16[2,512,256]{2,1,0:T(8,128)(2,1)S(1)}) custom-call(s32[8,2]{1,0:T(8,128)S(1)} %stack.242.place, bf16[512,1536]{1,0:T(8,128)(2,1)S(1)} %maximum_bitcast_fusion.left, ...), custom_call_target="tpu_custom_call" | custom-call | flops 3221225472 | bytes 10485760 | tf_op jit(solution)/shard_map/pallas_call | solution.py:100
  119.4 3.0 %collective-permute-start.23 = (bf16[768,256]{1,0:T(8,128)(2,1)S(1)}, bf16[768,256]{1,0:T(8,128)(2,1)S(1)}, u32[]{:S(2)}, u32[]{:S(2)}) collective-permute-start(bf16[768,256]{1,0:T(8,128)(2,1)S(1)} %get-tuple-element.43), channel_id=1, source_target_pairs={{0,2},{1,3},{2,0},{3,1},{4,6},{5,7},{6,4},{7,5},{8,10},{9,11},{10,... | collective-permute-start | bytes 1179656 | tf_op jit(solution)/shard_map/ppermute | solution.py:26
  122.4 6.5 %collective-permute-done.23 = bf16[768,256]{1,0:T(8,128)(2,1)S(1)} collective-permute-done((bf16[768,256]{1,0:T(8,128)(2,1)S(1)}, bf16[768,256]{1,0:T(8,128)(2,1)S(1)}, u32[]{:S(2)}, u32[]{:S(2)}) %collective-permute-start.23) | collective-permute-done | bytes 393248 | tf_op jit(solution)/shard_map/ppermute | solution.py:26
  129.0 4.1 %collective-permute-start.24 = (bf16[2,768,256]{2,1,0:T(8,128)(2,1)S(1)}, bf16[2,768,256]{2,1,0:T(8,128)(2,1)S(1)}, u32[]{:S(2)}, u32[]{:S(2)}) collective-permute-start(bf16[2,768,256]{2,1,0:T(8,128)(2,1)S(1)} %pad_maximum_fusion.4.refs_0_), channel_id=1, source_target_pairs={{0,12},{1,13},{2,14},{3,15},{4,0},{5,1},{6,2},{7,3},{8,4},{9,5},{1... | collective-permute-start | bytes 2359304 | tf_op jit(solution)/shard_map/ppermute | solution.py:26
  133.1 14.9 %collective-permute-done.24.refs_1_ = bf16[2,768,256]{2,1,0:T(8,128)(2,1)S(1)} collective-permute-done((bf16[2,768,256]{2,1,0:T(8,128)(2,1)S(1)}, bf16[2,768,256]{2,1,0:T(8,128)(2,1)S(1)}, u32[]{:S(2)}, u32[]{:S(2)}) %collective-permute-start.24) | collective-permute-done | bytes 786464 | tf_op jit(solution)/shard_map/ppermute | solution.py:26
  148.0 3.4 %collective-permute-done.25.refs_2_ = bf16[2,768,256]{2,1,0:T(8,128)(2,1)S(1)} collective-permute-done((bf16[2,768,256]{2,1,0:T(8,128)(2,1)S(1)}, bf16[2,768,256]{2,1,0:T(8,128)(2,1)S(1)}, u32[]{:S(2)}, u32[]{:S(2)}) %collective-permute-start.25) | collective-permute-done | bytes 786464 | tf_op jit(solution)/shard_map/ppermute | solution.py:26
  154.7 11.2 %collective-permute-done.26.refs_3_ = bf16[2,768,256]{2,1,0:T(8,128)(2,1)} collective-permute-done((bf16[2,768,256]{2,1,0:T(8,128)(2,1)}, bf16[2,768,256]{2,1,0:T(8,128)(2,1)}, u32[]{:S(2)}, u32[]{:S(2)}) %collective-permute-start.26) | collective-permute-done | bytes 786464 | tf_op jit(solution)/shard_map/ppermute | solution.py:26
  165.9 2.4 constant_dynamic-slice_fusion.3
  168.3 2.3 copy.96
  178.6 6.4 %shard_map.282 = (bf16[2,512,256]{2,1,0:T(8,128)(2,1)}, bf16[2,512,256]{2,1,0:T(8,128)(2,1)S(1)}, bf16[2,512,256]{2,1,0:T(8,128)(2,1)S(1)}, bf16[2,512,256]{2,1,0:T(8,128)(2,1)S(1)}) custom-call(s32[8,2]{1,0:T(8,128)S(1)} %stack.266.place, bf16[512,1536]{1,0:T(8,128)(2,1)S(1)} %maximum_bitcast_fusion.1.left, ...), custom_call_target="tpu_custom_call" | custom-call | flops 3221225472 | bytes 10485760 | tf_op jit(solution)/shard_map/pallas_call | solution.py:100
  188.1 2.9 %collective-permute-start.31 = (bf16[2,512,256]{2,1,0:T(8,128)(2,1)}, bf16[2,512,256]{2,1,0:T(8,128)(2,1)S(1)}, u32[]{:S(2)}, u32[]{:S(2)}) collective-permute-start(bf16[2,512,256]{2,1,0:T(8,128)(2,1)} %copy-done.13), channel_id=1, source_target_pairs={{0,48},{1,17},{2,50},{3,19},{4,52},{5,21},{6,54},{7,23},{8,56},{9,... | collective-permute-start | bytes 1572872 | tf_op jit(solution)/shard_map/ppermute | solution.py:26
  190.9 12.2 %collective-permute-done.32 = bf16[2,512,256]{2,1,0:T(8,128)(2,1)} collective-permute-done((bf16[2,512,256]{2,1,0:T(8,128)(2,1)}, bf16[2,512,256]{2,1,0:T(8,128)(2,1)}, u32[]{:S(2)}, u32[]{:S(2)}) %collective-permute-start.32) | collective-permute-done | bytes 524320 | tf_op jit(solution)/shard_map/ppermute | solution.py:26
  203.2 2.1 add_convert_fusion.1
  205.4 7.0 %collective-permute-done.36 = f32[5,128]{1,0:T(8,128)S(1)} collective-permute-done((f32[5,128]{1,0:T(8,128)S(1)}, f32[5,128]{1,0:T(8,128)S(1)}, u32[]{:S(2)}, u32[]{:S(2)}) %collective-permute-start.36) | collective-permute-done | bytes 2592 | tf_op jit(solution)/shard_map/ppermute | solution.py:26
  213.3 4.2 %collective-permute-done.37 = f32[5,128]{1,0:T(8,128)S(1)} collective-permute-done((f32[5,128]{1,0:T(8,128)S(1)}, f32[5,128]{1,0:T(8,128)S(1)}, u32[]{:S(2)}, u32[]{:S(2)}) %collective-permute-start.37) | collective-permute-done | bytes 2592 | tf_op jit(solution)/shard_map/ppermute | solution.py:26
  217.8 3.3 %collective-permute-done.38 = f32[5,128]{1,0:T(8,128)S(1)} collective-permute-done((f32[5,128]{1,0:T(8,128)S(1)}, f32[5,128]{1,0:T(8,128)S(1)}, u32[]{:S(2)}, u32[]{:S(2)}) %collective-permute-start.38) | collective-permute-done | bytes 2592 | tf_op jit(solution)/shard_map/ppermute | solution.py:26
  223.7 5.2 %collective-permute-done.34 = bf16[512,256]{1,0:T(8,128)(2,1)S(1)} collective-permute-done((bf16[512,256]{1,0:T(8,128)(2,1)S(1)}, bf16[512,256]{1,0:T(8,128)(2,1)S(1)}, u32[]{:S(2)}, u32[]{:S(2)}) %collective-permute-start.34) | collective-permute-done | bytes 262176 | tf_op jit(solution)/shard_map/ppermute | solution.py:26
  236.3 7.6 %shard_map.283 = bf16[1536,512]{1,0:T(8,128)(2,1)} custom-call(s32[10,2]{1,0:T(8,128)S(1)} %stack.215.place, bf16[512,2048]{1,0:T(8,128)(2,1)S(1)} %copy-done.12, bf16[1536,512]{1,0:T(8,128)(2,1)S(1)} %copy-done, bf16[2,768,256]{2,1,0:T(8,128)(2,1)S(1)} %copy-done.2, bf16[2,768,256]{2,1,0:T(8,128)(2,1)S(1)} %collective-permute-done.24.refs_1_, ...), custom_call_target="tpu_custom_call" | custom-call | flops 3221225472 | bytes 12582912 | tf_op jit(solution)/shard_map/pallas_call | solution.py:136
  (187 shorter events, 79.5 us)
Async XLA Ops:
  7.2 112.2 %all-gather.2.cloned.1.call-start = ((), (), s32[]{:S(2)}) async-start(), calls=%async_computation.1 | async-start | bytes 2359296 | tf_op jit(solution)/shard_map/all_gather | solution.py:221
  7.2 14.2 %collective-permute-start.3 = (bf16[256,512]{1,0:T(8,128)(2,1)}, bf16[256,512]{1,0:T(8,128)(2,1)}, u32[]{:S(2)}, u32[]{:S(2)}) collective-permute-start(bf16[256,512]{1,0:T(8,128)(2,1)} %param.31), channel_id=1, source_target_pairs={{0,64},{1,65},{2,66},{3,67},{4,68},{5,69},{6,70},{7,71},{8,72},{9,... | collective-permute-start | bytes 786440 | tf_op jit(solution)/shard_map/ppermute | solution.py:26
  18.5 12.9 %collective-permute-start.11 = (bf16[768,256]{1,0:T(8,128)(2,1)}, bf16[768,256]{1,0:T(8,128)(2,1)}, u32[]{:S(2)}, u32[]{:S(2)}) collective-permute-start(bf16[768,256]{1,0:T(8,128)(2,1)} %fusion.8), channel_id=1, source_target_pairs={{0,2},{1,3},{2,0},{3,1},{4,6},{5,7},{6,4},{7,5},{8,10},{9,11},{10,... | collective-permute-start | bytes 1179656 | tf_op jit(solution)/shard_map/ppermute | solution.py:26
  23.3 16.2 %collective-permute-start.7 = (bf16[2,256,512]{2,1,0:T(8,128)(2,1)}, bf16[2,256,512]{2,1,0:T(8,128)(2,1)}, u32[]{:S(2)}, u32[]{:S(2)}) collective-permute-start(bf16[2,256,512]{2,1,0:T(8,128)(2,1)} %pad_maximum_fusion.5), channel_id=1, source_target_pairs={{0,16},{1,17},{2,18},{3,19},{4,20},{5,21},{6,22},{7,23},{8,24},{9,... | collective-permute-start | bytes 1572872 | tf_op jit(solution)/shard_map/ppermute | solution.py:26
  25.2 15.8 %collective-permute-start.5 = (bf16[2,256,512]{2,1,0:T(8,128)(2,1)}, bf16[2,256,512]{2,1,0:T(8,128)(2,1)}, u32[]{:S(2)}, u32[]{:S(2)}) collective-permute-start(bf16[2,256,512]{2,1,0:T(8,128)(2,1)} %pad_maximum_fusion.5), channel_id=1, source_target_pairs={{0,48},{1,49},{2,50},{3,51},{4,52},{5,53},{6,54},{7,55},{8,56},{9,... | collective-permute-start | bytes 1572872 | tf_op jit(solution)/shard_map/ppermute | solution.py:26
  28.1 31.5 %collective-permute-start.2 = (bf16[768,512]{0,1:T(8,128)(2,1)S(1)}, bf16[768,512]{0,1:T(8,128)(2,1)}, u32[]{:S(2)}, u32[]{:S(2)}) collective-permute-start(bf16[768,512]{0,1:T(8,128)(2,1)S(1)} %get-tuple-element.90), channel_id=1, source_target_pairs={{0,1},{1,0},{2,3},{3,2},{4,5},{5,4},{6,7},{7,6},{8,9},{9,8},{10,11... | collective-permute-start | bytes 2359304 | tf_op jit(solution)/shard_map/ppermute | solution.py:26
  28.3 14.2 %collective-permute-start.4 = (bf16[2,256,512]{2,1,0:T(8,128)(2,1)}, bf16[2,256,512]{2,1,0:T(8,128)(2,1)S(1)}, u32[]{:S(2)}, u32[]{:S(2)}) collective-permute-start(bf16[2,256,512]{2,1,0:T(8,128)(2,1)} %pad_maximum_fusion.5), channel_id=1, source_target_pairs={{0,1},{1,0},{2,3},{3,2},{4,5},{5,4},{6,7},{7,6},{8,9},{9,8},{10,11... | collective-permute-start | bytes 1572872 | tf_op jit(solution)/shard_map/ppermute | solution.py:26
  33.4 24.9 %collective-permute-start.12 = (bf16[2,768,256]{2,1,0:T(8,128)(2,1)}, bf16[2,768,256]{2,1,0:T(8,128)(2,1)S(1)}, u32[]{:S(2)}, u32[]{:S(2)}) collective-permute-start(bf16[2,768,256]{2,1,0:T(8,128)(2,1)} %pad_maximum_fusion.3.refs_0_), channel_id=1, source_target_pairs={{0,12},{1,13},{2,14},{3,15},{4,0},{5,1},{6,2},{7,3},{8,4},{9,5},{1... | collective-permute-start | bytes 2359304 | tf_op jit(solution)/shard_map/ppermute | solution.py:26
  39.5 20.1 %collective-permute-start.13 = (bf16[2,768,256]{2,1,0:T(8,128)(2,1)}, bf16[2,768,256]{2,1,0:T(8,128)(2,1)S(1)}, u32[]{:S(2)}, u32[]{:S(2)}) collective-permute-start(bf16[2,768,256]{2,1,0:T(8,128)(2,1)} %pad_maximum_fusion.3.refs_0_), channel_id=1, source_target_pairs={{0,4},{1,5},{2,6},{3,7},{4,8},{5,9},{6,10},{7,11},{8,12},{9,13},{1... | collective-permute-start | bytes 2359304 | tf_op jit(solution)/shard_map/ppermute | solution.py:26
  42.4 10.5 %collective-permute-start.9 = (bf16[2,256,512]{2,1,0:T(8,128)(2,1)S(1)}, bf16[2,256,512]{2,1,0:T(8,128)(2,1)S(1)}, u32[]{:S(2)}, u32[]{:S(2)}) collective-permute-start(bf16[2,256,512]{2,1,0:T(8,128)(2,1)S(1)} %get-tuple-element.93), channel_id=1, source_target_pairs={{0,16},{1,49},{2,18},{3,51},{4,20},{5,53},{6,22},{7,55},{8,24},{9,... | collective-permute-start | bytes 1572872 | tf_op jit(solution)/shard_map/ppermute | solution.py:26
  59.5 170.2 %reduce-scatter.2.cloned.1.call-start = ((), (), s32[]{:S(2)}) async-start(), calls=%async_computation.2 | async-start | bytes 2359296 | tf_op jit(solution)/shard_map/reduce_scatter | solution.py:266
  62.9 16.6 %collective-permute-start.15 = (bf16[768,512]{0,1:T(8,128)(2,1)}, bf16[768,512]{0,1:T(8,128)(2,1)}, u32[]{:S(2)}, u32[]{:S(2)}) collective-permute-start(bf16[768,512]{0,1:T(8,128)(2,1)} %convolution_convert_fusion), channel_id=1, source_target_pairs={{0,4},{1,13},{2,6},{3,15},{4,8},{5,1},{6,10},{7,3},{8,12},{9,5},{1... | collective-permute-start | bytes 2359304 | tf_op jit(solution)/shard_map/ppermute | solution.py:26
  64.2 29.1 %collective-permute-start.18 = (bf16[2,768,256]{2,1,0:T(8,128)(2,1)}, bf16[2,768,256]{2,1,0:T(8,128)(2,1)}, u32[]{:S(2)}, u32[]{:S(2)}) collective-permute-start(bf16[2,768,256]{2,1,0:T(8,128)(2,1)} %broadcast_select_fusion.1), channel_id=1, source_target_pairs={{0,4},{1,13},{2,6},{3,15},{4,8},{5,1},{6,10},{7,3},{8,12},{9,5},{1... | collective-permute-start | bytes 2359304 | tf_op jit(solution)/shard_map/ppermute | solution.py:26
  69.0 24.3 %collective-permute-start.14 = (bf16[768,512]{0,1:T(8,128)(2,1)}, bf16[768,512]{0,1:T(8,128)(2,1)S(1)}, u32[]{:S(2)}, u32[]{:S(2)}) collective-permute-start(bf16[768,512]{0,1:T(8,128)(2,1)} %convolution_convert_fusion.1), channel_id=1, source_target_pairs={{0,12},{1,5},{2,14},{3,7},{4,0},{5,9},{6,2},{7,11},{8,4},{9,13},{1... | collective-permute-start | bytes 2359304 | tf_op jit(solution)/shard_map/ppermute | solution.py:26
  83.1 18.6 %collective-permute-start.16 = (bf16[768,512]{0,1:T(8,128)(2,1)}, bf16[768,512]{0,1:T(8,128)(2,1)}, u32[]{:S(2)}, u32[]{:S(2)}) collective-permute-start(bf16[768,512]{0,1:T(8,128)(2,1)} %add_convert_fusion), channel_id=1, source_target_pairs={{0,4},{1,13},{2,6},{3,15},{4,8},{5,1},{6,10},{7,3},{8,12},{9,5},{1... | collective-permute-start | bytes 2359304 | tf_op jit(solution)/shard_map/ppermute | solution.py:26
  85.9 21.8 %collective-permute-start.19 = (bf16[2,768,256]{2,1,0:T(8,128)(2,1)}, bf16[2,768,256]{2,1,0:T(8,128)(2,1)}, u32[]{:S(2)}, u32[]{:S(2)}) collective-permute-start(bf16[2,768,256]{2,1,0:T(8,128)(2,1)} %pad_maximum_fusion.3.refs_0_), channel_id=1, source_target_pairs={{0,1},{1,0},{2,3},{3,2},{4,5},{5,4},{6,7},{7,6},{8,9},{9,8},{10,11... | collective-permute-start | bytes 2359304 | tf_op jit(solution)/shard_map/ppermute | solution.py:26
  86.0 21.7 %collective-permute-start.20 = (bf16[2,768,256]{2,1,0:T(8,128)(2,1)S(1)}, bf16[2,768,256]{2,1,0:T(8,128)(2,1)}, u32[]{:S(2)}, u32[]{:S(2)}) collective-permute-start(bf16[2,768,256]{2,1,0:T(8,128)(2,1)S(1)} %collective-permute-done.12.refs_1_), channel_id=1, source_target_pairs={{0,1},{1,0},{2,3},{3,2},{4,5},{5,4},{6,7},{7,6},{8,9},{9,8},{10,11... | collective-permute-start | bytes 2359304 | tf_op jit(solution)/shard_map/ppermute | solution.py:26
  93.3 14.4 %collective-permute-start.21 = (bf16[2,768,256]{2,1,0:T(8,128)(2,1)S(1)}, bf16[2,768,256]{2,1,0:T(8,128)(2,1)}, u32[]{:S(2)}, u32[]{:S(2)}) collective-permute-start(bf16[2,768,256]{2,1,0:T(8,128)(2,1)S(1)} %collective-permute-done.13.refs_2_), channel_id=1, source_target_pairs={{0,1},{1,0},{2,3},{3,2},{4,5},{5,4},{6,7},{7,6},{8,9},{9,8},{10,11... | collective-permute-start | bytes 2359304 | tf_op jit(solution)/shard_map/ppermute | solution.py:26
  94.2 13.5 %collective-permute-start.22 = (bf16[2,768,256]{2,1,0:T(8,128)(2,1)}, bf16[2,768,256]{2,1,0:T(8,128)(2,1)}, u32[]{:S(2)}, u32[]{:S(2)}) collective-permute-start(bf16[2,768,256]{2,1,0:T(8,128)(2,1)} %collective-permute-done.18.refs_3_), channel_id=1, source_target_pairs={{0,1},{1,0},{2,3},{3,2},{4,5},{5,4},{6,7},{7,6},{8,9},{9,8},{10,11... | collective-permute-start | bytes 2359304 | tf_op jit(solution)/shard_map/ppermute | solution.py:26
  107.1 10.6 %collective-permute-start.17 = (bf16[768,256]{1,0:T(8,128)(2,1)}, bf16[768,256]{1,0:T(8,128)(2,1)}, u32[]{:S(2)}, u32[]{:S(2)}) collective-permute-start(bf16[768,256]{1,0:T(8,128)(2,1)} %bitcast.144), channel_id=1, source_target_pairs={{0,2},{1,3},{2,0},{3,1},{4,6},{5,7},{6,4},{7,5},{8,10},{9,11},{10,... | collective-permute-start | bytes 1179656 | tf_op jit(solution)/shard_map/ppermute | solution.py:26
  119.4 9.5 %collective-permute-start.23 = (bf16[768,256]{1,0:T(8,128)(2,1)S(1)}, bf16[768,256]{1,0:T(8,128)(2,1)S(1)}, u32[]{:S(2)}, u32[]{:S(2)}) collective-permute-start(bf16[768,256]{1,0:T(8,128)(2,1)S(1)} %get-tuple-element.43), channel_id=1, source_target_pairs={{0,2},{1,3},{2,0},{3,1},{4,6},{5,7},{6,4},{7,5},{8,10},{9,11},{10,... | collective-permute-start | bytes 1179656 | tf_op jit(solution)/shard_map/ppermute | solution.py:26
  129.0 19.0 %collective-permute-start.24 = (bf16[2,768,256]{2,1,0:T(8,128)(2,1)S(1)}, bf16[2,768,256]{2,1,0:T(8,128)(2,1)S(1)}, u32[]{:S(2)}, u32[]{:S(2)}) collective-permute-start(bf16[2,768,256]{2,1,0:T(8,128)(2,1)S(1)} %pad_maximum_fusion.4.refs_0_), channel_id=1, source_target_pairs={{0,12},{1,13},{2,14},{3,15},{4,0},{5,1},{6,2},{7,3},{8,4},{9,5},{1... | collective-permute-start | bytes 2359304 | tf_op jit(solution)/shard_map/ppermute | solution.py:26
  133.1 18.4 %collective-permute-start.25 = (bf16[2,768,256]{2,1,0:T(8,128)(2,1)S(1)}, bf16[2,768,256]{2,1,0:T(8,128)(2,1)S(1)}, u32[]{:S(2)}, u32[]{:S(2)}) collective-permute-start(bf16[2,768,256]{2,1,0:T(8,128)(2,1)S(1)} %pad_maximum_fusion.4.refs_0_), channel_id=1, source_target_pairs={{0,4},{1,5},{2,6},{3,7},{4,8},{5,9},{6,10},{7,11},{8,12},{9,13},{1... | collective-permute-start | bytes 2359304 | tf_op jit(solution)/shard_map/ppermute | solution.py:26
  152.4 13.5 %collective-permute-start.26 = (bf16[2,768,256]{2,1,0:T(8,128)(2,1)}, bf16[2,768,256]{2,1,0:T(8,128)(2,1)}, u32[]{:S(2)}, u32[]{:S(2)}) collective-permute-start(bf16[2,768,256]{2,1,0:T(8,128)(2,1)} %broadcast_select_fusion), channel_id=1, source_target_pairs={{0,4},{1,13},{2,6},{3,15},{4,8},{5,1},{6,10},{7,3},{8,12},{9,5},{1... | collective-permute-start | bytes 2359304 | tf_op jit(solution)/shard_map/ppermute | solution.py:26
  154.1 24.5 %collective-permute-start.27 = (bf16[2,768,256]{2,1,0:T(8,128)(2,1)S(1)}, bf16[2,768,256]{2,1,0:T(8,128)(2,1)}, u32[]{:S(2)}, u32[]{:S(2)}) collective-permute-start(bf16[2,768,256]{2,1,0:T(8,128)(2,1)S(1)} %pad_maximum_fusion.4.refs_0_), channel_id=1, source_target_pairs={{0,1},{1,0},{2,3},{3,2},{4,5},{5,4},{6,7},{7,6},{8,9},{9,8},{10,11... | collective-permute-start | bytes 2359304 | tf_op jit(solution)/shard_map/ppermute | solution.py:26
  154.1 24.4 %collective-permute-start.28 = (bf16[2,768,256]{2,1,0:T(8,128)(2,1)S(1)}, bf16[2,768,256]{2,1,0:T(8,128)(2,1)}, u32[]{:S(2)}, u32[]{:S(2)}) collective-permute-start(bf16[2,768,256]{2,1,0:T(8,128)(2,1)S(1)} %collective-permute-done.24.refs_1_), channel_id=1, source_target_pairs={{0,1},{1,0},{2,3},{3,2},{4,5},{5,4},{6,7},{7,6},{8,9},{9,8},{10,11... | collective-permute-start | bytes 2359304 | tf_op jit(solution)/shard_map/ppermute | solution.py:26
  154.6 23.9 %collective-permute-start.29 = (bf16[2,768,256]{2,1,0:T(8,128)(2,1)S(1)}, bf16[2,768,256]{2,1,0:T(8,128)(2,1)}, u32[]{:S(2)}, u32[]{:S(2)}) collective-permute-start(bf16[2,768,256]{2,1,0:T(8,128)(2,1)S(1)} %collective-permute-done.25.refs_2_), channel_id=1, source_target_pairs={{0,1},{1,0},{2,3},{3,2},{4,5},{5,4},{6,7},{7,6},{8,9},{9,8},{10,11... | collective-permute-start | bytes 2359304 | tf_op jit(solution)/shard_map/ppermute | solution.py:26
  165.9 12.6 %collective-permute-start.30 = (bf16[2,768,256]{2,1,0:T(8,128)(2,1)}, bf16[2,768,256]{2,1,0:T(8,128)(2,1)}, u32[]{:S(2)}, u32[]{:S(2)}) collective-permute-start(bf16[2,768,256]{2,1,0:T(8,128)(2,1)} %collective-permute-done.26.refs_3_), channel_id=1, source_target_pairs={{0,1},{1,0},{2,3},{3,2},{4,5},{5,4},{6,7},{7,6},{8,9},{9,8},{10,11... | collective-permute-start | bytes 2359304 | tf_op jit(solution)/shard_map/ppermute | solution.py:26
  186.6 16.6 %collective-permute-start.32 = (bf16[2,512,256]{2,1,0:T(8,128)(2,1)}, bf16[2,512,256]{2,1,0:T(8,128)(2,1)}, u32[]{:S(2)}, u32[]{:S(2)}) collective-permute-start(bf16[2,512,256]{2,1,0:T(8,128)(2,1)} %get-tuple-element.44), channel_id=1, source_target_pairs={{0,16},{1,49},{2,18},{3,51},{4,20},{5,53},{6,22},{7,55},{8,24},{9,... | collective-permute-start | bytes 1572872 | tf_op jit(solution)/shard_map/ppermute | solution.py:26
  188.1 33.1 %collective-permute-start.31 = (bf16[2,512,256]{2,1,0:T(8,128)(2,1)}, bf16[2,512,256]{2,1,0:T(8,128)(2,1)S(1)}, u32[]{:S(2)}, u32[]{:S(2)}) collective-permute-start(bf16[2,512,256]{2,1,0:T(8,128)(2,1)} %copy-done.13), channel_id=1, source_target_pairs={{0,48},{1,17},{2,50},{3,19},{4,52},{5,21},{6,54},{7,23},{8,56},{9,... | collective-permute-start | bytes 1572872 | tf_op jit(solution)/shard_map/ppermute | solution.py:26
  205.3 15.9 %collective-permute-start.33 = (bf16[2,512,256]{2,1,0:T(8,128)(2,1)}, bf16[2,512,256]{2,1,0:T(8,128)(2,1)}, u32[]{:S(2)}, u32[]{:S(2)}) collective-permute-start(bf16[2,512,256]{2,1,0:T(8,128)(2,1)} %add_convert_fusion.1), channel_id=1, source_target_pairs={{0,16},{1,49},{2,18},{3,51},{4,20},{5,53},{6,22},{7,55},{8,24},{9,... | collective-permute-start | bytes 1572872 | tf_op jit(solution)/shard_map/ppermute | solution.py:26
  205.3 7.1 %collective-permute-start.36 = (f32[5,128]{1,0:T(8,128)S(1)}, f32[5,128]{1,0:T(8,128)S(1)}, u32[]{:S(2)}, u32[]{:S(2)}) collective-permute-start(f32[5,128]{1,0:T(8,128)S(1)} %maximum_bitcast_fusion.2), channel_id=1, source_target_pairs={{0,16},{1,17},{2,18},{3,19},{4,20},{5,21},{6,22},{7,23},{8,24},{9,... | collective-permute-start | bytes 7688 | tf_op jit(solution)/shard_map/ppermute | solution.py:26
  (36 other events, 397.5 us)
Sparse Core Ops, SparseCore 0:
  59.7 41.2 all-gather.1
  154.2 41.4 reduce-scatter.1
